TPU v7x, 32 devices: a whole 2x2x4 slice. The times are simulated.
32 devices in a mesh: cls: 4 (over y, x), ptl: 8 (over z, core).
Axes of the slice: x: 2, y: 2, z: 4, core: 2. Of those that a mesh axis runs over, the one named last changes fastest.
Arguments:
- references: bfloat16 [4, 256, 4096], P('cls', 'ptl')
- particles: bfloat16 [16384, 4096], P(('cls', 'ptl'))
- class_ids: int32 [16384], P(('cls', 'ptl')), may hold values from 0 to 3, as said below
- orient_ids: int32 [16384], P(('cls', 'ptl')), may hold values from 0 to 255
- offsets: int32 [16384], P(('cls', 'ptl')), may hold values from -3 to 3
- weights: float32 [16384], P(('cls', 'ptl'))
Outputs:
- class_sums: float32 [4, 4096], P('cls', 'ptl')
Inputs may be any that keep to these rules, and one draw needn't show every extreme that they name: `class_ids`: every class is the class of some particle; populations are uneven.
All inputs are finite; a program needn't handle non-finite values.
Results may differ from a plain program's by a relative error of at most 0.0028.
Values may be sent and summed in bfloat16 or wider, within the bound.
A program may use at most 64 MiB of HBM per device.

v0:
```python
import math

import jax
import jax.numpy as jnp
from jax import lax
from jax.sharding import PartitionSpec as P

NX = 64
SHIFT = 3


def body(references, particles, class_ids, orient_ids, offsets, weights):
    n_cls = lax.axis_size("cls")
    n_ptl = lax.axis_size("ptl")
    per_owner, local_ori, voxels = references.shape
    orients = local_ori * n_ptl
    classes = per_owner * n_cls
    count = particles.shape[0]
    scale = 1.0 / math.sqrt(voxels)
    class_block = lax.all_gather(references, "ptl", axis=1, tiled=True)
    piece = lax.all_gather(class_block, "cls", axis=0, tiled=True)
    rows = piece.reshape(piece.shape[0] * orients, voxels)
    place = jnp.arange(rows.shape[0], dtype=jnp.int32)
    top = jnp.full((count,), -1e30, jnp.float32)
    scores = (
        lax.dot_general(
            particles, rows, (((1,), (1,)), ((), ())), preferred_element_type=jnp.float32
        )
        * scale
    )
    newtop = jnp.maximum(top, jnp.max(scores, axis=1))
    total = jnp.sum(jnp.exp(scores - newtop[:, None]), axis=1)
    picked = (class_ids[:, None] == (place // orients)[None, :]) & (
        orient_ids[:, None] == (place % orients)[None, :]
    )
    chosen = jnp.sum(jnp.where(picked, scores, 0.0), axis=1)
    top, total, chosen = (newtop, total, chosen)
    gain = (weights * (classes * orients) * jnp.exp(chosen - top) / total).astype(jnp.bfloat16)
    member = class_ids[None, :] == jnp.arange(classes, dtype=jnp.int32)[:, None]
    partial_sums = jnp.zeros((classes, voxels), jnp.float32)
    for step in range(-SHIFT, SHIFT + 1):
        coef = jnp.where(
            member & (offsets[None, :] == step), gain[None, :], jnp.zeros((), jnp.bfloat16)
        )
        moved = jnp.dot(coef, particles, preferred_element_type=jnp.float32)
        moved = jnp.roll(moved.reshape(classes, voxels // NX, NX), step, axis=2).reshape(
            classes, voxels
        )
        partial_sums = partial_sums + moved
    owned = lax.psum_scatter(partial_sums, "cls", scatter_dimension=0, tiled=True)
    owned = lax.psum_scatter(owned, "ptl", scatter_dimension=1, tiled=True)
    population = count * n_cls * n_ptl / classes
    return owned / jnp.sqrt(jnp.float32(population))


def solution(mesh):
    placed = (
        P("cls", "ptl", None),
        P(("cls", "ptl"), None),
        P(("cls", "ptl")),
        P(("cls", "ptl")),
        P(("cls", "ptl")),
        P(("cls", "ptl")),
    )
    return jax.shard_map(
        body, mesh=mesh, in_specs=placed, out_specs=P("cls", "ptl"), check_vma=False
    )
```

profile of v0, /device:TPU:0, one launch (start us, length us, event | category | flops | bytes accessed | tf_op | source)
XLA Modules:
  0.0 250.1 jit_solution(951586413182705998)
XLA Ops:
  6.5 0.7 all-gather.3.cloned.1.call-update
  7.3 33.5 %all-gather.3.cloned.1.call-done = bf16[1,256,4096]{2,1,0:T(8,128)(2,1)} async-done(((bf16[1,32,4096]{2,1,0:T(8,128)(2,1)}), bf16[1,256,4096]{2,1,0:T(8,128)(2,1)}) %all-gather.3.cloned.1.call-update) | async-done | bytes 2097168 | tf_op jit(solution)/shard_map/all_gather | solution.py:20
  40.9 0.7 broadcast_compare_fusion.3
  41.6 88.2 %all-gather.5.cloned.1.call-done = bf16[4,256,4096]{2,1,0:T(8,128)(2,1)} async-done(((bf16[1,256,4096]{2,1,0:T(8,128)(2,1)}), bf16[4,256,4096]{2,1,0:T(8,128)(2,1)}) %all-gather.5.cloned.1.call-update) | async-done | bytes 8388624 | tf_op jit(solution)/shard_map/all_gather | solution.py:21
  129.8 9.6 %select_reduce_fusion = (f32[512]{0:T(512)S(1)}, f32[512]{0:T(512)S(1)}, f32[512,1024]{1,0:T(8,128)S(1)}) fusion(s32[1024]{0:T(1024)S(1)} %get-tuple-element.15, s32[1024]{0:T(1024)S(1)} %get-tuple-element.16, s32[512]{0:T(512)} %param.9, s32[512]{0:T(512)} %param.8, bf16[512,4096]{1,0:T(8,128)(2,1)} %param.7, bf16[1024,4096]{1,0:T(8,128)(2,1)} %bitcast.27), kind=kOutput, calls=%fused_computation.5 | convolution fusion | flops 4298636288 | bytes 14696448 | tf_op jit(solution)/shard_map/dot_general | solution.py:26
  139.4 0.5 exponential_reduce_fusion
  140.0 0.7 fusion.35
  140.6 0.1 reshape.81
  140.9 2.8 %fusion.33 = f32[4,4096]{1,0:T(4,128)S(1)} fusion(bf16[512,4096]{1,0:T(8,128)(2,1)} %param.7, s32[512]{0:T(512)S(1)} %copy-done.1, pred[512]{0:T(512)(128)(4,1)S(1)} %get-tuple-element.10, bf16[512]{0:T(512)(128)(2,1)S(1)} %fusion.66), kind=kOutput, calls=%fused_computation.41 | convolution fusion | flops 16783360 | bytes 4263424 | tf_op jit(solution)/shard_map/dot_general | solution.py:45
  143.7 0.1 reshape.82
  143.9 2.8 %fusion.31 = f32[4,4096]{1,0:T(4,128)S(1)} fusion(bf16[512,4096]{1,0:T(8,128)(2,1)} %param.7, s32[512]{0:T(512)S(1)} %copy-done.1, pred[512]{0:T(512)(128)(4,1)S(1)} %get-tuple-element.9, bf16[512]{0:T(512)(128)(2,1)S(1)} %fusion.66), kind=kOutput, calls=%fused_computation.40 | convolution fusion | flops 16783360 | bytes 4263424 | tf_op jit(solution)/shard_map/dot_general | solution.py:45
  146.8 0.1 reshape.83
  147.0 0.2 fusion.3
  147.2 0.1 add.44
  147.3 2.8 %fusion.28 = f32[4,4096]{1,0:T(4,128)S(1)} fusion(bf16[512,4096]{1,0:T(8,128)(2,1)} %param.7, s32[512]{0:T(512)S(1)} %copy-done.1, pred[512]{0:T(512)(128)(4,1)S(1)} %get-tuple-element.8, bf16[512]{0:T(512)(128)(2,1)S(1)} %fusion.66), kind=kOutput, calls=%fused_computation.39 | convolution fusion | flops 16783360 | bytes 4263424 | tf_op jit(solution)/shard_map/dot_general | solution.py:45
  150.2 0.1 reshape.84
  150.5 0.1 reshape.85
  150.6 2.8 %fusion.26 = f32[4,4096]{1,0:T(4,128)S(1)} fusion(bf16[512,4096]{1,0:T(8,128)(2,1)} %param.7, s32[512]{0:T(512)S(1)} %copy-done.1, pred[512]{0:T(512)(128)(4,1)S(1)} %get-tuple-element.13, bf16[512]{0:T(512)(128)(2,1)S(1)} %fusion.66), kind=kOutput, calls=%fused_computation.38 | convolution fusion | flops 16783360 | bytes 4263424 | tf_op jit(solution)/shard_map/dot_general | solution.py:45
  153.4 0.1 reshape.86
  153.7 0.1 pad_maximum_fusion.1
  153.8 0.1 reshape.87
  153.9 2.8 %fusion.24 = f32[4,4096]{1,0:T(4,128)S(1)} fusion(bf16[512,4096]{1,0:T(8,128)(2,1)} %param.7, s32[512]{0:T(512)S(1)} %copy-done.1, pred[512]{0:T(512)(128)(4,1)S(1)} %get-tuple-element.12, bf16[512]{0:T(512)(128)(2,1)S(1)} %fusion.66), kind=kOutput, calls=%fused_computation.37 | convolution fusion | flops 16783360 | bytes 4263424 | tf_op jit(solution)/shard_map/dot_general | solution.py:45
  156.7 0.1 reshape.88
  157.1 0.1 reshape.89
  157.2 3.5 %fusion.2 = f32[4,4096]{1,0:T(4,128)} fusion(f32[4,4096]{1,0:T(4,128)S(1)} %reshape.89, f32[4,4096]{1,0:T(4,128)S(1)} %reshape.87, f32[4,4096]{1,0:T(4,128)S(1)} %reshape.85, f32[4,4096]{1,0:T(4,128)S(1)} %add.44, bf16[512,4096]{1,0:T(8,128)(2,1)} %param.7, s32[512]{0:T(512)S(1)} %copy-done.1, pred[512]{0:T(512)(128)(4,1)S(1)} %get-tuple-element.7, ...), kind=kOutput, calls=%fused_computation.3 | convolution fusion | flops 16848896 | bytes 4525568 | tf_op jit(solution)/shard_map/dot_general | solution.py:45
  160.8 0.6 dynamic-slice
  161.4 41.0 %all-reduce.3.cloned.1.call-done = f32[4,4096]{1,0:T(4,128)} async-done(((f32[4,4096]{1,0:T(4,128)}), f32[4,4096]{1,0:T(4,128)}) %all-reduce.3.cloned.1.call-update) | async-done | bytes 65552
  202.4 1.5 constant_dynamic-slice_fusion
  203.9 2.0 copy.7
  205.9 36.0 %reduce-scatter.4.cloned.1.call-done = f32[512,1]{1,0:T(8,128)} async-done(((f32[4096,1]{1,0:T(8,128)}), f32[512,1]{1,0:T(8,128)}) %reduce-scatter.4.cloned.1.call-update) | async-done | bytes 2064
  241.9 1.1 copy.8
  243.0 0.6 broadcast_multiply_fusion
  (26 shorter events, 1.0 us)
Async XLA Ops:
  6.5 34.3 %all-gather.3.cloned.1.call-start = ((), (), s32[]{:S(2)}) async-start(), calls=%async_computation.1 | async-start | bytes 2359296 | tf_op jit(solution)/shard_map/all_gather | solution.py:20
  7.3 122.5 %all-gather.5.cloned.1.call-start = ((), (), s32[]{:S(2)}) async-start(), calls=%async_computation.2 | async-start | bytes 10485760 | tf_op jit(solution)/shard_map/all_gather | solution.py:21
  40.8 161.5 %all-reduce.3.cloned.1.call-start = ((), (), s32[]{:S(2)}) async-start(), calls=%async_computation.4 | async-start | bytes 131072
  129.8 10.2 %copy-start.2 = (f32[512]{0:T(512)S(1)}, f32[512]{0:T(512)}, u32[]{:S(2)}) copy-start(f32[512]{0:T(512)} %param.11) | copy-start | bytes 6148
  129.8 10.2 %copy-start = (bf16[512,4096]{1,0:T(8,128)(2,1)S(1)}, bf16[512,4096]{1,0:T(8,128)(2,1)}, u32[]{:S(2)}) copy-start(bf16[512,4096]{1,0:T(8,128)(2,1)} %param.7) | copy-start | bytes 12582916
  129.8 10.2 %copy-start.1 = (s32[512]{0:T(512)S(1)}, s32[512]{0:T(512)}, u32[]{:S(2)}) copy-start(s32[512]{0:T(512)} %param.8) | copy-start | bytes 6148
  153.9 6.9 %copy-start.3 = (u32[32]{0:T(128)S(1)}, u32[32]{0:T(128)}, u32[]{:S(2)}) copy-start(u32[32]{0:T(128)} %constant.59) | copy-start | bytes 388
  160.7 81.2 %reduce-scatter.4.cloned.1.call-start = ((), (), s32[]{:S(2)}) async-start(), calls=%async_computation.3 | async-start | bytes 2359296
Sparse Core Ops, SparseCore 0:
  9.0 31.7 all-gather.2
  42.6 87.0 all-gather.4
  160.8 41.4 all-reduce.2
  206.0 35.8 reduce-scatter.3
where the time goes:
time: 251 us; the launch traced here: 250 us
  waiting for transfers between devices  199 us (79%)
  matrix products  28 us (11%)
  between operations  13.3 us (5%)
  local copies, waits for them, and re-layouts  6.89 us (3%)
    all_gather x1, waiting for transfers between devices, body(): piece = lax.all_gather(class_block, 'cls', axis=0, tiled=True)  88.2 us
    unnamed x6, waiting for transfers between devices  77.8 us
    all_gather x1, waiting for transfers between devices, body(): class_block = lax.all_gather(references, 'ptl', axis=1, tiled=True)  33.5 us
    dot_general x7, matrix products, body(): moved = jnp.dot(coef, particles, preferred_element_type=jnp.float32)  18.4 us
    dot_general x1, matrix products, body(): lax.dot_general(particles, rows, (((1,), (1,)), ((), ())), preferred_elem...  9.62 us
    unnamed x12, local copies, waits for them, and re-layouts  5.14 us
  transfers between devices with their start and end apart: 4, of which 4 were waited for; matrix products, arithmetic and copies ran while one was open for 1% of the time, Pallas kernels for 0%

commit v1 on v0

--- a/solution.py
+++ b/solution.py
@@ -1,12 +1,351 @@
+import functools
 import math
 
 import jax
 import jax.numpy as jnp
 from jax import lax
+from jax.experimental import pallas as pl
+from jax.experimental.pallas import tpu as pltpu
 from jax.sharding import PartitionSpec as P
 
 NX = 64
 SHIFT = 3
+MESH = pl.DeviceIdType.MESH
+
+PLAN = (
+    (
+        (
+            (0, 0, 1, 0), (0, 0, 0, 1), (0, 0, 0, 2), (0, 0, 0, 0), (0, 0, 1, 1),
+            (0, 0, 1, 2), (0, 1, 0, -1), (2, 0, 0, -1), (1, 0, 1, -1), (2, 0, 0, 0),
+            (1, 0, 1, 1), (0, 1, 0, 1), (0, 1, 1, -1), (2, 0, 1, -1), (1, 0, 0, -1),
+            (0, 1, 1, 0),
+        ),
+        (
+            (0, 1, 0, 0), (0, 1, 1, 1), (0, 2, 0, -1), (3, 0, 1, -1), (3, 0, 0, -1),
+            (3, 0, 1, 2), (3, 0, 0, 2), (0, 2, 0, 0), (0, 2, 0, 1), (0, 2, 1, -1),
+            (2, 1, 0, -1), (1, 1, 1, -1), (0, 2, 1, 0), (0, 2, 1, 1), (0, 3, 0, -1),
+            (2, 1, 1, -1), (1, 1, 0, -1),
+        ),
+        (
+            (2, 1, 0, 0), (1, 1, 1, 1), (0, 3, 1, -1), (2, 2, 0, -1), (1, 2, 0, -1),
+            (0, 3, 0, 0), (0, 3, 0, 1), (3, 2, 0, -1), (2, 2, 1, -1), (1, 2, 1, -1),
+            (0, 3, 1, 0), (0, 3, 1, 1), (3, 3, 1, -1), (3, 1, 1, -1), (3, 1, 0, -1),
+        ),
+        (
+            (3, 2, 1, -1), (2, 3, 0, -1), (1, 3, 0, -1), (3, 3, 0, -1), (2, 3, 1, -1),
+            (1, 3, 1, -1),
+        ),
+    ),
+    (
+        (
+            (0, 1, 1, 0), (0, 1, 0, 1), (0, 1, 0, 2), (0, 1, 0, 3), (0, 1, 0, 0),
+            (0, 1, 1, 1), (0, 1, 1, 2), (0, 1, 1, 3), (0, 0, 0, -1), (0, 2, 0, -1),
+            (2, 1, 0, -1), (1, 1, 1, -1), (0, 0, 0, 0), (0, 2, 0, 1), (0, 0, 0, 2),
+            (0, 2, 0, 3), (0, 0, 0, 1), (0, 0, 1, -1), (0, 2, 1, -1), (2, 1, 1, -1),
+            (1, 1, 0, -1), (0, 2, 1, 0), (0, 0, 1, 2), (0, 2, 1, 3),
+        ),
+        (
+            (1, 1, 1, 1), (0, 3, 0, -1), (2, 2, 0, -1), (1, 0, 0, -1), (2, 2, 0, 0),
+            (0, 3, 0, 3), (0, 2, 0, 0), (0, 3, 1, -1), (2, 0, 0, -1), (1, 2, 1, -1),
+            (1, 2, 1, 1), (0, 3, 1, 3), (3, 0, 1, -1), (3, 0, 1, 2), (2, 1, 0, 0),
+            (0, 0, 1, 1), (3, 1, 1, -1), (3, 2, 0, -1), (3, 2, 0, 3), (3, 0, 0, -1),
+            (3, 0, 0, 2), (3, 3, 1, -1), (0, 0, 1, 0), (0, 2, 1, 1), (3, 3, 1, 3),
+            (3, 2, 1, -1), (1, 2, 0, -1), (3, 3, 0, -1),
+        ),
+        (
+            (0, 3, 0, 0), (0, 3, 0, 1), (3, 2, 1, 3), (2, 0, 1, -1), (3, 1, 0, -1),
+            (0, 3, 1, 0), (0, 3, 1, 1), (3, 3, 0, 3), (2, 2, 1, -1), (1, 0, 1, -1),
+        ),
+        (
+            (2, 3, 0, -1), (1, 3, 0, -1), (2, 3, 1, -1), (1, 3, 1, -1),
+        ),
+    ),
+)
+
+GROUPS = (
+    (
+        ((0, 0), (0, 1), (2, 0), (1, 0)),
+        ((3, 0), (0, 2), (2, 1), (1, 1)),
+        ((0, 3), (2, 2), (1, 2), (3, 1)),
+        ((3, 2), (2, 3), (1, 3), (3, 3)),
+    ),
+    (
+        ((0, 1), (0, 0), (0, 2), (2, 1)),
+        ((1, 1), (0, 3), (3, 0), (1, 2)),
+        ((3, 2), (3, 3), (2, 0), (3, 1)),
+        ((2, 2), (1, 0), (2, 3), (1, 3)),
+    ),
+)
+DEPTH = 1024
+ROWS = 8
+
+
+def kernel(
+    orients, population,
+    refs, parts, cid, oid, off, wts, out,
+    rows, pv, top_s, tot_s, cho_s, part, recv1, send2, recv2,
+    local_sem, ici_sem, sib_sem, send_sem, r1_sem, r2_sem, s1_sem, s2_sem,
+):
+    n_cls, n_ptl = part.shape[0], part.shape[1]
+    voxels = refs.shape[2]
+    half = pv.shape[1]
+    cls, ptl = lax.axis_index("cls"), lax.axis_index("ptl")
+    core, z = ptl % 2, ptl // 2
+    far = z // 2
+    sign = 1 - 2 * far
+    place = z + far * (3 - 2 * z)
+    along_x = cls + 1 - 2 * (cls % 2)
+    along_y = cls + 2 - 4 * (cls // 2)
+    column = (cls, along_x, along_y, 3 - cls)
+    sibling = (cls, ptl + 1 - 2 * core)
+    ways = (
+        (along_x, ptl),
+        (along_y, ptl),
+        (cls, ptl + 2 * sign),
+        (cls, ptl - 2 * sign),
+    )
+
+    def pair(q, zz):
+        return column[q] * 4 + zz + far * (3 - 2 * zz)
+
+    barrier = pltpu.get_barrier_semaphore()
+    for q in (1, 2, 3):
+        pl.semaphore_signal(barrier, inc=1, device_id=(column[q], ptl), device_id_type=MESH)
+    for o in range(1, n_ptl):
+        pl.semaphore_signal(
+            barrier, inc=1, device_id=(cls, lax.rem(ptl + o, n_ptl)), device_id_type=MESH
+        )
+    loads = [
+        pltpu.make_async_copy(parts.at[pl.ds(i * half, half)], pv.at[i], local_sem.at[i])
+        for i in range(2)
+    ]
+    own = cls * 4 + z
+    for h in range(2):
+        loads.append(
+            pltpu.make_async_copy(
+                refs.at[0, pl.ds(16 * h, 16)], rows.at[own, core, h], local_sem.at[2 + h]
+            )
+        )
+    for load in loads:
+        load.start()
+    pl.semaphore_wait(barrier, 3 + n_ptl - 1)
+
+    def send(src, p, h, way):
+        target, recv, idx = (
+            (sibling, sib_sem, 4) if way == 4 else (ways[way], ici_sem, way)
+        )
+        pltpu.make_async_remote_copy(
+            src_ref=src,
+            dst_ref=rows.at[p, core, h],
+            send_sem=send_sem.at[idx],
+            recv_sem=recv.at[p, h],
+            device_id=target,
+            device_id_type=MESH,
+        ).start()
+
+    def run(section):
+        for q, zz, h, way in section:
+            p = pair(q, zz)
+            block = rows.at[p, core, h]
+            if way < 0:
+                pltpu.make_async_copy(block, block, ici_sem.at[p, h]).wait()
+                send(block, p, h, 4)
+            elif q == 0 and p_own(zz):
+                send(refs.at[0, pl.ds(16 * h, 16)], p, h, way)
+            else:
+                send(block, p, h, way)
+
+    top_s[...] = jnp.full(top_s.shape, -jnp.inf, jnp.float32)
+    tot_s[...] = jnp.zeros(tot_s.shape, jnp.float32)
+    cho_s[...] = jnp.zeros(cho_s.shape, jnp.float32)
+
+    for s in range(4):
+        for zc in range(2):
+            def p_own(zz, zc=zc):
+                return zz == zc
+
+            def branch(s=s, zc=zc):
+                if s == 0:
+                    first = [e for e in PLAN[zc][0] if e[0] == 0 and e[1] == zc]
+                    rest = [e for e in PLAN[zc][0] if not (e[0] == 0 and e[1] == zc)]
+                    run(first)
+                    for h in range(2):
+                        send(refs.at[0, pl.ds(16 * h, 16)], own, h, 4)
+                    run(rest)
+                else:
+                    run(PLAN[zc][s])
+
+            pl.when(place == zc)(branch)
+        if s == 0:
+            for load in loads:
+                load.wait()
+        group = []
+        for a, b in zip(GROUPS[0][s], GROUPS[1][s]):
+            group.append(jnp.where(place == 0, pair(*a), pair(*b)))
+        for p in group:
+            for h in range(2):
+                block = rows.at[p, 1 - core, h]
+                pltpu.make_async_copy(block, block, sib_sem.at[p, h]).wait()
+
+        def scores(n, _, group=group):
+            acc = jnp.zeros((4 * 64, half), jnp.float32)
+            for k in range(0, voxels, DEPTH):
+                lhs = jnp.concatenate(
+                    [rows[p, :, :, :, k : k + DEPTH].reshape(64, DEPTH) for p in group], axis=0
+                )
+                acc += lax.dot_general(
+                    lhs,
+                    pv[n, :, k : k + DEPTH],
+                    (((1,), (1,)), ((), ())),
+                    preferred_element_type=jnp.float32,
+                )
+            sc = acc * (1.0 / math.sqrt(voxels))
+            cols = pl.ds(pl.multiple_of(n * half, half), half)
+            old = top_s[:, cols]
+            new = jnp.maximum(old, jnp.max(sc, axis=0, keepdims=True))
+            top_s[:, cols] = new
+            tot_s[:, cols] = tot_s[:, cols] * jnp.exp(old - new) + jnp.sum(
+                jnp.exp(sc - new), axis=0, keepdims=True
+            )
+            wanted = cid[:, cols] * orients + oid[:, cols]
+            inner = lax.broadcasted_iota(jnp.int32, (64, half), 0)
+            picked = jnp.zeros((1, half), jnp.float32)
+            for i, p in enumerate(group):
+                mine = inner == wanted - p * 64
+                picked += jnp.sum(
+                    jnp.where(mine, sc[64 * i : 64 * i + 64], 0.0), axis=0, keepdims=True
+                )
+            cho_s[:, cols] += picked
+            return _
+
+        lax.fori_loop(0, 2, scores, 0)
+
+    gain = wts[...] * (n_cls * orients) * jnp.exp(cho_s[...] - top_s[...]) / tot_s[...]
+    gain = gain.astype(jnp.bfloat16).astype(jnp.float32)
+    code = (off[...] + SHIFT) * ROWS + cid[...]
+    steps = 2 * SHIFT + 1
+    which = lax.broadcasted_iota(jnp.int32, (steps * ROWS, 2 * half), 0)
+    coef = jnp.where(which == code, gain, 0.0).astype(jnp.bfloat16)
+    width = voxels // n_ptl
+    lane = lax.broadcasted_iota(jnp.int32, (ROWS, 128), 1) % NX
+    for j in range(n_ptl):
+        pixels = pv[:, :, j * width : (j + 1) * width].reshape(2 * half, width)
+        moved = jnp.dot(coef, pixels, preferred_element_type=jnp.float32)
+        for v in range(width // 128):
+            total = jnp.zeros((ROWS, 128), jnp.float32)
+            for i, step in enumerate(range(-SHIFT, SHIFT + 1)):
+                a = moved[i * ROWS : (i + 1) * ROWS, v * 128 : (v + 1) * 128]
+                if step == 0:
+                    total += a
+                    continue
+                inside = pltpu.roll(a, step % 128, 1)
+                across = pltpu.roll(a, (step + NX) % 128, 1)
+                keep = lane >= step if step > 0 else lane < NX + step
+                total += jnp.where(keep, inside, across)
+            for c in range(n_cls):
+                part[c, j : j + 1, v * 128 : (v + 1) * 128] = total[c : c + 1]
+
+    copies = []
+    for q in (1, 2, 3):
+        copies.append(
+            pltpu.make_async_remote_copy(
+                src_ref=part.at[column[q]],
+                dst_ref=recv1.at[q - 1],
+                send_sem=s1_sem.at[q - 1],
+                recv_sem=r1_sem.at[q - 1],
+                device_id=(column[q], ptl),
+                device_id_type=MESH,
+            )
+        )
+        copies[-1].start()
+    for copy in copies:
+        copy.wait_recv()
+    mine = part[cls] + recv1[0] + recv1[1] + recv1[2]
+    for j in range(n_ptl):
+        send2[j] = mine[j : j + 1]
+    for o in range(1, n_ptl):
+        to = lax.rem(ptl + o, n_ptl)
+        copies.append(
+            pltpu.make_async_remote_copy(
+                src_ref=send2.at[to],
+                dst_ref=recv2.at[o - 1],
+                send_sem=s2_sem.at[o - 1],
+                recv_sem=r2_sem.at[o - 1],
+                device_id=(cls, to),
+                device_id_type=MESH,
+            )
+        )
+        copies[-1].start()
+    total = send2[ptl]
+    for o in range(1, n_ptl):
+        copies[2 + o].wait_recv()
+        total += recv2[o - 1]
+    out[...] = total / jnp.sqrt(jnp.float32(population))
+    for copy in copies:
+        copy.wait_send()
+
+    def sent(count, idx):
+        gone = rows.at[pl.ds(0, count), 0]
+        pltpu.make_async_copy(gone, gone, send_sem.at[idx]).wait()
+
+    sent(5, 0)
+    sent(5, 1)
+    sent(16, 4)
+
+    @pl.when(place == 0)
+    def _():
+        sent(2, 2)
+
+    @pl.when(place == 1)
+    def _():
+        sent(3, 2)
+        sent(5, 3)
+
+
+def fused(references, particles, class_ids, orient_ids, offsets, weights):
+    n_cls = lax.axis_size("cls")
+    n_ptl = lax.axis_size("ptl")
+    _, local_ori, voxels = references.shape
+    count = particles.shape[0]
+    orients = local_ori * n_ptl
+    population = count * n_ptl
+    line = [x.reshape(1, count) for x in (class_ids, orient_ids, offsets, weights)]
+    f32 = jnp.float32
+    vmem = pl.BlockSpec(memory_space=pltpu.VMEM)
+    hbm = pl.BlockSpec(memory_space=pl.ANY)
+    return pl.pallas_call(
+        functools.partial(kernel, orients, population),
+        out_shape=jax.ShapeDtypeStruct((1, voxels // n_ptl), f32),
+        in_specs=[hbm, hbm, vmem, vmem, vmem, vmem],
+        out_specs=vmem,
+        scratch_shapes=[
+            pltpu.VMEM((n_cls * n_ptl // 2, 2, 2, local_ori // 2, voxels), references.dtype),
+            pltpu.VMEM((2, count // 2, voxels), particles.dtype),
+            pltpu.VMEM((1, count), f32),
+            pltpu.VMEM((1, count), f32),
+            pltpu.VMEM((1, count), f32),
+            pltpu.VMEM((n_cls, n_ptl, voxels // n_ptl), f32),
+            pltpu.VMEM((n_cls - 1, n_ptl, voxels // n_ptl), f32),
+            pltpu.VMEM((n_ptl, 1, voxels // n_ptl), f32),
+            pltpu.VMEM((n_ptl - 1, 1, voxels // n_ptl), f32),
+            pltpu.SemaphoreType.DMA((4,)),
+            pltpu.SemaphoreType.DMA((n_cls * n_ptl // 2, 2)),
+            pltpu.SemaphoreType.DMA((n_cls * n_ptl // 2, 2)),
+            pltpu.SemaphoreType.DMA((5,)),
+            pltpu.SemaphoreType.DMA((n_cls - 1,)),
+            pltpu.SemaphoreType.DMA((n_ptl - 1,)),
+            pltpu.SemaphoreType.DMA((n_cls - 1,)),
+            pltpu.SemaphoreType.DMA((n_ptl - 1,)),
+        ],
+        compiler_params=pltpu.CompilerParams(
+            collective_id=0, has_side_effects=True, vmem_limit_bytes=40 * 1024 * 1024
+        ),
+        cost_estimate=pl.CostEstimate(
+            flops=2 * count * voxels * n_cls * orients,
+            bytes_accessed=2 * voxels * (count + n_cls * orients),
+            transcendentals=count * n_cls * orients,
+        ),
+    )(references, particles, *line)
 
 
 def body(references, particles, class_ids, orient_ids, offsets, weights):
@@ -62,6 +401,11 @@
         P(("cls", "ptl")),
         P(("cls", "ptl")),
     )
+    planned = mesh.shape["cls"] == 4 and mesh.shape["ptl"] == 8
     return jax.shard_map(
-        body, mesh=mesh, in_specs=placed, out_specs=P("cls", "ptl"), check_vma=False
+        fused if planned else body,
+        mesh=mesh,
+        in_specs=placed,
+        out_specs=P("cls", "ptl"),
+        check_vma=False,
     )

time: 251 us -> 54.7 us (0.22)
  waiting for transfers between devices: 199 us -> 0 us
  Pallas kernels: 0 us -> 48 us
  matrix products: 28 us -> 0 us
  between operations: 13.3 us -> 0.02 us
    all_gather x2 -> x0, waiting for transfers between devices: 122 us -> none  [the longest x1 88.2 us: body(): piece = lax.all_gather(class_block, 'cls', axis=0, tiled=True)]
    unnamed x6 -> x0, waiting for transfers between devices: 77.8 us -> none
    pallas_call x0 -> x1, Pallas kernels: none -> 48 us  [fused(): pl.pallas_call(functools.partial(kernel, orients, population), out_shape=...]
    dot_general x8 -> x0, matrix products: 28 us -> none  [the longest x7 18.4 us: body(): moved = jnp.dot(coef, particles, preferred_element_type=jnp.float32)]
    unnamed x12 -> x13, local copies, waits for them, and re-layouts: 5.14 us -> 6.44 us
  transfers between devices with their start and end apart: 4 -> 0, of which waited for: 4 -> 0; matrix products, arithmetic and copies ran while one was open for 1% -> 0% of each run, Pallas kernels for 0% -> 0%
where the time goes in v1:
time: 54.7 us; the launch traced here: 54.4 us
  Pallas kernels  48 us (88%)
  local copies, waits for them, and re-layouts  6.44 us (12%)
    pallas_call x1, Pallas kernels, fused(): pl.pallas_call(functools.partial(kernel, orients, population), out_shape=...  48 us
    unnamed x13, local copies, waits for them, and re-layouts  6.44 us

profile of v1, /device:TPU:0, one launch (start us, length us, event | category | flops | bytes accessed | tf_op | source)
XLA Modules:
  0.0 54.4 jit_solution(14993437166932534626)
XLA Ops:
  0.0 0.0 copy-start
  0.0 2.2 %copy-done = bf16[512,4096]{1,0:T(8,128)(2,1)S(1)} copy-done((bf16[512,4096]{1,0:T(8,128)(2,1)S(1)}, bf16[512,4096]{1,0:T(8,128)(2,1)}, u32[]{:S(2)}) %copy-start) | copy-done | bytes 4194328
  2.2 0.0 copy-start.1
  2.2 0.9 %copy-done.1 = bf16[1,32,4096]{2,1,0:T(8,128)(2,1)S(1)} copy-done((bf16[1,32,4096]{2,1,0:T(8,128)(2,1)S(1)}, bf16[1,32,4096]{2,1,0:T(8,128)(2,1)}, u32[]{:S(2)}) %copy-start.1) | copy-done | bytes 262168
  3.1 0.0 copy-start.2
  3.1 0.7 %copy-done.2 = s32[512]{0:T(512)S(1)} copy-done((s32[512]{0:T(512)S(1)}, s32[512]{0:T(512)}, u32[]{:S(2)}) %copy-start.2) | copy-done | bytes 2072
  3.8 0.0 copy-start.3
  3.8 0.7 %copy-done.3 = s32[512]{0:T(512)S(1)} copy-done((s32[512]{0:T(512)S(1)}, s32[512]{0:T(512)}, u32[]{:S(2)}) %copy-start.3) | copy-done | bytes 2072
  4.5 0.0 copy-start.4
  4.5 0.7 %copy-done.4 = s32[512]{0:T(512)S(1)} copy-done((s32[512]{0:T(512)S(1)}, s32[512]{0:T(512)}, u32[]{:S(2)}) %copy-start.4) | copy-done | bytes 2072
  5.2 0.0 copy-start.5
  5.2 0.7 %copy-done.5 = f32[512]{0:T(512)S(1)} copy-done((f32[512]{0:T(512)S(1)}, f32[512]{0:T(512)}, u32[]{:S(2)}) %copy-start.5) | copy-done | bytes 2072
  5.9 48.0 %shard_map.64 = f32[1,512]{1,0:T(1,128)S(1)} custom-call(bf16[1,32,4096]{2,1,0:T(8,128)(2,1)S(1)} %copy-done.1, bf16[512,4096]{1,0:T(8,128)(2,1)S(1)} %copy-done, s32[1,512]{1,0:T(1,128)S(1)} %bitcast.4, s32[1,512]{1,0:T(1,128)S(1)} %bitcast.5, s32[1,512]{1,0:T(1,128)S(1)} %bitcast.6, f32[1,512]{1,0:T(1,128)S(1)} %bitcast.7), custom_call_target="tpu_custom_call" | custom-call | flops 4294967296 | bytes 12582912 | tf_op jit(solution)/shard_map/pallas_call | solution.py:316
  53.8 0.6 %copy.8 = f32[1,512]{1,0:T(1,128)} copy(f32[1,512]{1,0:T(1,128)S(1)} %shard_map.64) | data formatting | bytes 4096
Async XLA Ops:
  0.0 2.2 %copy-start = (bf16[512,4096]{1,0:T(8,128)(2,1)S(1)}, bf16[512,4096]{1,0:T(8,128)(2,1)}, u32[]{:S(2)}) copy-start(bf16[512,4096]{1,0:T(8,128)(2,1)} %parts.1) | copy-start | bytes 12582916
  2.2 0.9 %copy-start.1 = (bf16[1,32,4096]{2,1,0:T(8,128)(2,1)S(1)}, bf16[1,32,4096]{2,1,0:T(8,128)(2,1)}, u32[]{:S(2)}) copy-start(bf16[1,32,4096]{2,1,0:T(8,128)(2,1)} %refs.1) | copy-start | bytes 786436
  3.1 0.7 %copy-start.2 = (s32[512]{0:T(512)S(1)}, s32[512]{0:T(512)}, u32[]{:S(2)}) copy-start(s32[512]{0:T(512)} %param.8) | copy-start | bytes 6148
  3.8 0.7 %copy-start.3 = (s32[512]{0:T(512)S(1)}, s32[512]{0:T(512)}, u32[]{:S(2)}) copy-start(s32[512]{0:T(512)} %param.9) | copy-start | bytes 6148
  4.5 0.7 %copy-start.4 = (s32[512]{0:T(512)S(1)}, s32[512]{0:T(512)}, u32[]{:S(2)}) copy-start(s32[512]{0:T(512)} %param.10) | copy-start | bytes 6148
  5.2 0.7 %copy-start.5 = (f32[512]{0:T(512)S(1)}, f32[512]{0:T(512)}, u32[]{:S(2)}) copy-start(f32[512]{0:T(512)} %param.11) | copy-start | bytes 6148

commit v2 on v1

--- a/solution.py
+++ b/solution.py
@@ -15,49 +15,78 @@
 PLAN = (
     (
         (
-            (0, 0, 1, 0), (0, 0, 0, 1), (0, 0, 0, 2), (0, 0, 0, 0), (0, 0, 1, 1),
-            (0, 0, 1, 2), (0, 1, 0, -1), (2, 0, 0, -1), (1, 0, 1, -1), (2, 0, 0, 0),
-            (1, 0, 1, 1), (0, 1, 0, 1), (0, 1, 1, -1), (2, 0, 1, -1), (1, 0, 0, -1),
-            (0, 1, 1, 0),
-        ),
-        (
-            (0, 1, 0, 0), (0, 1, 1, 1), (0, 2, 0, -1), (3, 0, 1, -1), (3, 0, 0, -1),
-            (3, 0, 1, 2), (3, 0, 0, 2), (0, 2, 0, 0), (0, 2, 0, 1), (0, 2, 1, -1),
-            (2, 1, 0, -1), (1, 1, 1, -1), (0, 2, 1, 0), (0, 2, 1, 1), (0, 3, 0, -1),
-            (2, 1, 1, -1), (1, 1, 0, -1),
+            (0, 0, 1, 0), (0, 0, 0, 1), (0, 0, 0, 2), (0, 0, 0, 0), (0, 0, 1, 1), (0, 0, 1, 2),
+        ),
+        (
+            (0, 1, 0, -1), (2, 0, 0, -1), (1, 0, 1, -1), (2, 0, 0, 0), (1, 0, 1, 1),
+        ),
+        (
+            (0, 1, 0, 1), (0, 1, 1, -1), (2, 0, 1, -1), (1, 0, 0, -1), (0, 1, 1, 0),
+        ),
+        (
+            (0, 1, 0, 0), (0, 1, 1, 1), (0, 2, 0, -1), (3, 0, 1, -1), (3, 0, 0, -1), (3, 0, 1, 2),
+            (3, 0, 0, 2),
+        ),
+        (
+            (0, 2, 0, 0), (0, 2, 0, 1), (0, 2, 1, -1), (2, 1, 0, -1), (1, 1, 1, -1),
+        ),
+        (
+            (0, 2, 1, 0), (0, 2, 1, 1), (0, 3, 0, -1), (2, 1, 1, -1), (1, 1, 0, -1),
         ),
         (
             (2, 1, 0, 0), (1, 1, 1, 1), (0, 3, 1, -1), (2, 2, 0, -1), (1, 2, 0, -1),
+        ),
+        (
             (0, 3, 0, 0), (0, 3, 0, 1), (3, 2, 0, -1), (2, 2, 1, -1), (1, 2, 1, -1),
+        ),
+        (
             (0, 3, 1, 0), (0, 3, 1, 1), (3, 3, 1, -1), (3, 1, 1, -1), (3, 1, 0, -1),
         ),
         (
-            (3, 2, 1, -1), (2, 3, 0, -1), (1, 3, 0, -1), (3, 3, 0, -1), (2, 3, 1, -1),
-            (1, 3, 1, -1),
+            (3, 2, 1, -1), (2, 3, 0, -1), (1, 3, 0, -1),
+        ),
+        (
+            (3, 3, 0, -1), (2, 3, 1, -1), (1, 3, 1, -1),
         ),
     ),
     (
         (
-            (0, 1, 1, 0), (0, 1, 0, 1), (0, 1, 0, 2), (0, 1, 0, 3), (0, 1, 0, 0),
-            (0, 1, 1, 1), (0, 1, 1, 2), (0, 1, 1, 3), (0, 0, 0, -1), (0, 2, 0, -1),
-            (2, 1, 0, -1), (1, 1, 1, -1), (0, 0, 0, 0), (0, 2, 0, 1), (0, 0, 0, 2),
-            (0, 2, 0, 3), (0, 0, 0, 1), (0, 0, 1, -1), (0, 2, 1, -1), (2, 1, 1, -1),
-            (1, 1, 0, -1), (0, 2, 1, 0), (0, 0, 1, 2), (0, 2, 1, 3),
-        ),
-        (
-            (1, 1, 1, 1), (0, 3, 0, -1), (2, 2, 0, -1), (1, 0, 0, -1), (2, 2, 0, 0),
-            (0, 3, 0, 3), (0, 2, 0, 0), (0, 3, 1, -1), (2, 0, 0, -1), (1, 2, 1, -1),
-            (1, 2, 1, 1), (0, 3, 1, 3), (3, 0, 1, -1), (3, 0, 1, 2), (2, 1, 0, 0),
-            (0, 0, 1, 1), (3, 1, 1, -1), (3, 2, 0, -1), (3, 2, 0, 3), (3, 0, 0, -1),
-            (3, 0, 0, 2), (3, 3, 1, -1), (0, 0, 1, 0), (0, 2, 1, 1), (3, 3, 1, 3),
-            (3, 2, 1, -1), (1, 2, 0, -1), (3, 3, 0, -1),
+            (0, 1, 1, 0), (0, 1, 0, 1), (0, 1, 0, 2), (0, 1, 0, 3), (0, 1, 0, 0), (0, 1, 1, 1),
+            (0, 1, 1, 2), (0, 1, 1, 3),
+        ),
+        (
+            (0, 0, 0, -1), (0, 2, 0, -1), (2, 1, 0, -1), (1, 1, 1, -1), (0, 0, 0, 0), (0, 2, 0, 1),
+            (0, 0, 0, 2), (0, 2, 0, 3),
+        ),
+        (
+            (0, 0, 0, 1), (0, 0, 1, -1), (0, 2, 1, -1), (2, 1, 1, -1), (1, 1, 0, -1), (0, 2, 1, 0),
+            (0, 0, 1, 2), (0, 2, 1, 3),
+        ),
+        (
+            (1, 1, 1, 1), (0, 3, 0, -1), (2, 2, 0, -1), (1, 0, 0, -1), (2, 2, 0, 0), (0, 3, 0, 3),
+        ),
+        (
+            (0, 2, 0, 0), (0, 3, 1, -1), (2, 0, 0, -1), (1, 2, 1, -1), (1, 2, 1, 1), (0, 3, 1, 3),
+            (3, 0, 1, -1), (3, 0, 1, 2),
+        ),
+        (
+            (2, 1, 0, 0), (0, 0, 1, 1), (3, 1, 1, -1), (3, 2, 0, -1), (3, 2, 0, 3), (3, 0, 0, -1),
+            (3, 0, 0, 2), (3, 3, 1, -1),
+        ),
+        (
+            (0, 0, 1, 0), (0, 2, 1, 1), (3, 3, 1, 3), (3, 2, 1, -1), (1, 2, 0, -1), (3, 3, 0, -1),
         ),
         (
             (0, 3, 0, 0), (0, 3, 0, 1), (3, 2, 1, 3), (2, 0, 1, -1), (3, 1, 0, -1),
+        ),
+        (
             (0, 3, 1, 0), (0, 3, 1, 1), (3, 3, 0, 3), (2, 2, 1, -1), (1, 0, 1, -1),
         ),
         (
-            (2, 3, 0, -1), (1, 3, 0, -1), (2, 3, 1, -1), (1, 3, 1, -1),
+            (2, 3, 0, -1), (1, 3, 0, -1),
+        ),
+        (
+            (2, 3, 1, -1), (1, 3, 1, -1),
         ),
     ),
 )
@@ -76,14 +105,15 @@
         ((2, 2), (1, 0), (2, 3), (1, 3)),
     ),
 )
+UNITS = ((), (), ((0, 0),), ((0, 1),), (), (), ((1, 0),), ((1, 1),), ((2, 0),), ((2, 1),), ((3, 0), (3, 1)))
 DEPTH = 1024
 ROWS = 8
 
 
 def kernel(
     orients, population,
-    refs, parts, cid, oid, off, wts, out,
-    rows, pv, top_s, tot_s, cho_s, part, recv1, send2, recv2,
+    refs, parts, cid_in, oid_in, off_in, wts_in, out,
+    rows, pv, cid, oid, off, wts, top_s, tot_s, cho_s, part, recv1, send2, recv2,
     local_sem, ici_sem, sib_sem, send_sem, r1_sem, r2_sem, s1_sem, s2_sem,
 ):
     n_cls, n_ptl = part.shape[0], part.shape[1]
@@ -126,6 +156,8 @@
                 refs.at[0, pl.ds(16 * h, 16)], rows.at[own, core, h], local_sem.at[2 + h]
             )
         )
+    for i, (a, b) in enumerate(((cid_in, cid), (oid_in, oid), (off_in, off), (wts_in, wts))):
+        loads.append(pltpu.make_async_copy(a, b, local_sem.at[4 + i]))
     for load in loads:
         load.start()
     pl.semaphore_wait(barrier, 3 + n_ptl - 1)
@@ -143,14 +175,14 @@
             device_id_type=MESH,
         ).start()
 
-    def run(section):
+    def run(section, zc):
         for q, zz, h, way in section:
             p = pair(q, zz)
             block = rows.at[p, core, h]
             if way < 0:
                 pltpu.make_async_copy(block, block, ici_sem.at[p, h]).wait()
                 send(block, p, h, 4)
-            elif q == 0 and p_own(zz):
+            elif q == 0 and zz == zc:
                 send(refs.at[0, pl.ds(16 * h, 16)], p, h, way)
             else:
                 send(block, p, h, way)
@@ -159,66 +191,60 @@
     tot_s[...] = jnp.zeros(tot_s.shape, jnp.float32)
     cho_s[...] = jnp.zeros(cho_s.shape, jnp.float32)
 
-    for s in range(4):
+    def scores(n, group):
+        acc = jnp.zeros((len(group) * 64, half), jnp.float32)
+        for k in range(0, voxels, DEPTH):
+            lhs = jnp.concatenate(
+                [rows[p, :, :, :, k : k + DEPTH].reshape(64, DEPTH) for p in group], axis=0
+            )
+            acc += lax.dot_general(
+                lhs,
+                pv[n, :, k : k + DEPTH],
+                (((1,), (1,)), ((), ())),
+                preferred_element_type=jnp.float32,
+            )
+        sc = acc * (1.0 / math.sqrt(voxels))
+        cols = pl.ds(n * half, half)
+        old = top_s[:, cols]
+        new = jnp.maximum(old, jnp.max(sc, axis=0, keepdims=True))
+        top_s[:, cols] = new
+        tot_s[:, cols] = tot_s[:, cols] * jnp.exp(old - new) + jnp.sum(
+            jnp.exp(sc - new), axis=0, keepdims=True
+        )
+        wanted = cid[:, cols] * orients + oid[:, cols]
+        inner = lax.broadcasted_iota(jnp.int32, (64, half), 0)
+        picked = jnp.zeros((1, half), jnp.float32)
+        for i, p in enumerate(group):
+            mine = inner == wanted - p * 64
+            picked += jnp.sum(
+                jnp.where(mine, sc[64 * i : 64 * i + 64], 0.0), axis=0, keepdims=True
+            )
+        cho_s[:, cols] += picked
+
+    groups = [
+        [jnp.where(place == 0, pair(*a), pair(*b)) for a, b in zip(first, second)]
+        for first, second in zip(*GROUPS)
+    ]
+    for s, units in enumerate(UNITS):
         for zc in range(2):
-            def p_own(zz, zc=zc):
-                return zz == zc
 
             def branch(s=s, zc=zc):
+                run(PLAN[zc][s], zc)
                 if s == 0:
-                    first = [e for e in PLAN[zc][0] if e[0] == 0 and e[1] == zc]
-                    rest = [e for e in PLAN[zc][0] if not (e[0] == 0 and e[1] == zc)]
-                    run(first)
                     for h in range(2):
                         send(refs.at[0, pl.ds(16 * h, 16)], own, h, 4)
-                    run(rest)
-                else:
-                    run(PLAN[zc][s])
 
             pl.when(place == zc)(branch)
         if s == 0:
             for load in loads:
                 load.wait()
-        group = []
-        for a, b in zip(GROUPS[0][s], GROUPS[1][s]):
-            group.append(jnp.where(place == 0, pair(*a), pair(*b)))
-        for p in group:
-            for h in range(2):
-                block = rows.at[p, 1 - core, h]
-                pltpu.make_async_copy(block, block, sib_sem.at[p, h]).wait()
-
-        def scores(n, _, group=group):
-            acc = jnp.zeros((4 * 64, half), jnp.float32)
-            for k in range(0, voxels, DEPTH):
-                lhs = jnp.concatenate(
-                    [rows[p, :, :, :, k : k + DEPTH].reshape(64, DEPTH) for p in group], axis=0
-                )
-                acc += lax.dot_general(
-                    lhs,
-                    pv[n, :, k : k + DEPTH],
-                    (((1,), (1,)), ((), ())),
-                    preferred_element_type=jnp.float32,
-                )
-            sc = acc * (1.0 / math.sqrt(voxels))
-            cols = pl.ds(pl.multiple_of(n * half, half), half)
-            old = top_s[:, cols]
-            new = jnp.maximum(old, jnp.max(sc, axis=0, keepdims=True))
-            top_s[:, cols] = new
-            tot_s[:, cols] = tot_s[:, cols] * jnp.exp(old - new) + jnp.sum(
-                jnp.exp(sc - new), axis=0, keepdims=True
-            )
-            wanted = cid[:, cols] * orients + oid[:, cols]
-            inner = lax.broadcasted_iota(jnp.int32, (64, half), 0)
-            picked = jnp.zeros((1, half), jnp.float32)
-            for i, p in enumerate(group):
-                mine = inner == wanted - p * 64
-                picked += jnp.sum(
-                    jnp.where(mine, sc[64 * i : 64 * i + 64], 0.0), axis=0, keepdims=True
-                )
-            cho_s[:, cols] += picked
-            return _
-
-        lax.fori_loop(0, 2, scores, 0)
+        for g, n in units:
+            if n == 0:
+                for p in groups[g]:
+                    for h in range(2):
+                        block = rows.at[p, 1 - core, h]
+                        pltpu.make_async_copy(block, block, sib_sem.at[p, h]).wait()
+            scores(n, groups[g])
 
     gain = wts[...] * (n_cls * orients) * jnp.exp(cho_s[...] - top_s[...]) / tot_s[...]
     gain = gain.astype(jnp.bfloat16).astype(jnp.float32)
@@ -316,11 +342,12 @@
     return pl.pallas_call(
         functools.partial(kernel, orients, population),
         out_shape=jax.ShapeDtypeStruct((1, voxels // n_ptl), f32),
-        in_specs=[hbm, hbm, vmem, vmem, vmem, vmem],
+        in_specs=[hbm] * 6,
         out_specs=vmem,
         scratch_shapes=[
             pltpu.VMEM((n_cls * n_ptl // 2, 2, 2, local_ori // 2, voxels), references.dtype),
             pltpu.VMEM((2, count // 2, voxels), particles.dtype),
+            *[pltpu.VMEM((1, count), x.dtype) for x in line],
             pltpu.VMEM((1, count), f32),
             pltpu.VMEM((1, count), f32),
             pltpu.VMEM((1, count), f32),
@@ -328,7 +355,7 @@
             pltpu.VMEM((n_cls - 1, n_ptl, voxels // n_ptl), f32),
             pltpu.VMEM((n_ptl, 1, voxels // n_ptl), f32),
             pltpu.VMEM((n_ptl - 1, 1, voxels // n_ptl), f32),
-            pltpu.SemaphoreType.DMA((4,)),
+            pltpu.SemaphoreType.DMA((8,)),
             pltpu.SemaphoreType.DMA((n_cls * n_ptl // 2, 2)),
             pltpu.SemaphoreType.DMA((n_cls * n_ptl // 2, 2)),
             pltpu.SemaphoreType.DMA((5,)),
@@ -338,7 +365,7 @@
             pltpu.SemaphoreType.DMA((n_ptl - 1,)),
         ],
         compiler_params=pltpu.CompilerParams(
-            collective_id=0, has_side_effects=True, vmem_limit_bytes=40 * 1024 * 1024
+            collective_id=0, has_side_effects=True, vmem_limit_bytes=60 * 1024 * 1024
         ),
         cost_estimate=pl.CostEstimate(
             flops=2 * count * voxels * n_cls * orients,

time: 54.7 us -> 49.6 us (0.907)
  local copies, waits for them, and re-layouts: 6.44 us -> 1.26 us
    unnamed x13 -> x1, local copies, waits for them, and re-layouts: 6.44 us -> 1.26 us
where the time goes in v2:
time: 49.6 us; the launch traced here: 49.4 us
  Pallas kernels  48.2 us (97%)
  local copies, waits for them, and re-layouts  1.26 us (3%)
    pallas_call x1, Pallas kernels, fused(): pl.pallas_call(functools.partial(kernel, orients, population), out_shape=...  48.2 us
    unnamed x1, local copies, waits for them, and re-layouts  1.26 us

profile of v2, /device:TPU:0, one launch (start us, length us, event | category | flops | bytes accessed | tf_op | source)
XLA Modules:
  0.0 49.4 jit_solution(7598299388619021695)
XLA Ops:
  0.0 48.2 %shard_map.64 = f32[1,512]{1,0:T(1,128)} custom-call(bf16[1,32,4096]{2,1,0:T(8,128)(2,1)} %refs.1, bf16[512,4096]{1,0:T(8,128)(2,1)} %parts.1, s32[1,512]{1,0:T(1,128)} %bitcast.4, s32[1,512]{1,0:T(1,128)} %bitcast.5, s32[1,512]{1,0:T(1,128)} %bitcast.6, f32[1,512]{1,0:T(1,128)} %bitcast.7), custom_call_target="tpu_custom_call" | custom-call | flops 4294967296 | bytes 12582912 | tf_op jit(solution)/shard_map/pallas_call | solution.py:342
  48.2 1.3 %copy.8 = f32[1,512]{1,0:T(1,128)} copy(f32[1,512]{1,0:T(1,128)} %shard_map.64) | data formatting | bytes 4096

commit v3 on v2

--- a/solution.py
+++ b/solution.py
@@ -113,7 +113,7 @@
 def kernel(
     orients, population,
     refs, parts, cid_in, oid_in, off_in, wts_in, out,
-    rows, pv, cid, oid, off, wts, top_s, tot_s, cho_s, part, recv1, send2, recv2,
+    rows, pv, turned, cid, oid, off, wts, top_s, tot_s, cho_s, part, recv1, send2, recv2,
     local_sem, ici_sem, sib_sem, send_sem, r1_sem, r2_sem, s1_sem, s2_sem,
 ):
     n_cls, n_ptl = part.shape[0], part.shape[1]
@@ -199,8 +199,8 @@
             )
             acc += lax.dot_general(
                 lhs,
-                pv[n, :, k : k + DEPTH],
-                (((1,), (1,)), ((), ())),
+                turned[n, k : k + DEPTH, :],
+                (((1,), (0,)), ((), ())),
                 preferred_element_type=jnp.float32,
             )
         sc = acc * (1.0 / math.sqrt(voxels))
@@ -238,6 +238,14 @@
         if s == 0:
             for load in loads:
                 load.wait()
+        if s < 2:
+
+            def turn(k, carry, n=s):
+                span = pl.ds(pl.multiple_of(k * half, half), half)
+                turned[n, span, :] = pv[n, :, span].T
+                return carry
+
+            lax.fori_loop(0, voxels // half, turn, 0)
         for g, n in units:
             if n == 0:
                 for p in groups[g]:
@@ -347,6 +355,7 @@
         scratch_shapes=[
             pltpu.VMEM((n_cls * n_ptl // 2, 2, 2, local_ori // 2, voxels), references.dtype),
             pltpu.VMEM((2, count // 2, voxels), particles.dtype),
+            pltpu.VMEM((2, voxels, count // 2), particles.dtype),
             *[pltpu.VMEM((1, count), x.dtype) for x in line],
             pltpu.VMEM((1, count), f32),
             pltpu.VMEM((1, count), f32),

time: 49.6 us -> 49.6 us (level)
  no operation moved by 1% of the time
where the time goes in v3:
time: 49.6 us; the launch traced here: 49.5 us
  Pallas kernels  48.2 us (97%)
  local copies, waits for them, and re-layouts  1.26 us (3%)
    pallas_call x1, Pallas kernels, fused(): pl.pallas_call(functools.partial(kernel, orients, population), out_shape=...  48.2 us
    unnamed x1, local copies, waits for them, and re-layouts  1.26 us

profile of v3, /device:TPU:0, one launch (start us, length us, event | category | flops | bytes accessed | tf_op | source)
XLA Modules:
  0.0 49.5 jit_solution(13090889096299830094)
XLA Ops:
  0.0 48.2 %shard_map.64 = f32[1,512]{1,0:T(1,128)} custom-call(bf16[1,32,4096]{2,1,0:T(8,128)(2,1)} %refs.1, bf16[512,4096]{1,0:T(8,128)(2,1)} %parts.1, s32[1,512]{1,0:T(1,128)} %bitcast.4, s32[1,512]{1,0:T(1,128)} %bitcast.5, s32[1,512]{1,0:T(1,128)} %bitcast.6, f32[1,512]{1,0:T(1,128)} %bitcast.7), custom_call_target="tpu_custom_call" | custom-call | flops 4294967296 | bytes 12582912 | tf_op jit(solution)/shard_map/pallas_call | solution.py:350
  48.2 1.3 %copy.8 = f32[1,512]{1,0:T(1,128)} copy(f32[1,512]{1,0:T(1,128)} %shard_map.64) | data formatting | bytes 4096

commit v4 on v2

--- a/solution.py
+++ b/solution.py
@@ -21,26 +21,25 @@
             (0, 1, 0, -1), (2, 0, 0, -1), (1, 0, 1, -1), (2, 0, 0, 0), (1, 0, 1, 1),
         ),
         (
-            (0, 1, 0, 1), (0, 1, 1, -1), (2, 0, 1, -1), (1, 0, 0, -1), (0, 1, 1, 0),
-        ),
-        (
-            (0, 1, 0, 0), (0, 1, 1, 1), (0, 2, 0, -1), (3, 0, 1, -1), (3, 0, 0, -1), (3, 0, 1, 2),
-            (3, 0, 0, 2),
-        ),
-        (
-            (0, 2, 0, 0), (0, 2, 0, 1), (0, 2, 1, -1), (2, 1, 0, -1), (1, 1, 1, -1),
-        ),
-        (
-            (0, 2, 1, 0), (0, 2, 1, 1), (0, 3, 0, -1), (2, 1, 1, -1), (1, 1, 0, -1),
-        ),
-        (
-            (2, 1, 0, 0), (1, 1, 1, 1), (0, 3, 1, -1), (2, 2, 0, -1), (1, 2, 0, -1),
-        ),
-        (
-            (0, 3, 0, 0), (0, 3, 0, 1), (3, 2, 0, -1), (2, 2, 1, -1), (1, 2, 1, -1),
-        ),
-        (
-            (0, 3, 1, 0), (0, 3, 1, 1), (3, 3, 1, -1), (3, 1, 1, -1), (3, 1, 0, -1),
+            (0, 1, 1, -1), (2, 0, 1, -1), (1, 0, 0, -1), (0, 1, 1, 0), (0, 1, 0, 1),
+        ),
+        (
+            (0, 2, 0, -1), (3, 0, 1, -1), (3, 0, 0, -1), (3, 0, 1, 2), (0, 1, 0, 0), (0, 1, 1, 1),
+        ),
+        (
+            (3, 0, 0, 2), (0, 2, 1, -1), (2, 1, 0, -1), (1, 1, 1, -1), (0, 2, 0, 0), (0, 2, 0, 1),
+        ),
+        (
+            (0, 3, 0, -1), (2, 1, 1, -1), (1, 1, 0, -1), (0, 2, 1, 0), (0, 2, 1, 1),
+        ),
+        (
+            (0, 3, 1, -1), (2, 2, 0, -1), (1, 2, 0, -1), (2, 1, 0, 0), (1, 1, 1, 1),
+        ),
+        (
+            (3, 2, 0, -1), (2, 2, 1, -1), (1, 2, 1, -1), (0, 3, 0, 0), (0, 3, 0, 1),
+        ),
+        (
+            (3, 3, 1, -1), (3, 1, 1, -1), (3, 1, 0, -1), (0, 3, 1, 0), (0, 3, 1, 1),
         ),
         (
             (3, 2, 1, -1), (2, 3, 0, -1), (1, 3, 0, -1),
@@ -59,28 +58,28 @@
             (0, 0, 0, 2), (0, 2, 0, 3),
         ),
         (
-            (0, 0, 0, 1), (0, 0, 1, -1), (0, 2, 1, -1), (2, 1, 1, -1), (1, 1, 0, -1), (0, 2, 1, 0),
+            (0, 0, 1, -1), (0, 2, 1, -1), (2, 1, 1, -1), (1, 1, 0, -1), (0, 2, 1, 0), (0, 0, 0, 1),
             (0, 0, 1, 2), (0, 2, 1, 3),
         ),
         (
-            (1, 1, 1, 1), (0, 3, 0, -1), (2, 2, 0, -1), (1, 0, 0, -1), (2, 2, 0, 0), (0, 3, 0, 3),
-        ),
-        (
-            (0, 2, 0, 0), (0, 3, 1, -1), (2, 0, 0, -1), (1, 2, 1, -1), (1, 2, 1, 1), (0, 3, 1, 3),
+            (0, 3, 0, -1), (2, 2, 0, -1), (1, 0, 0, -1), (2, 2, 0, 0), (1, 1, 1, 1), (0, 3, 0, 3),
+        ),
+        (
+            (0, 3, 1, -1), (2, 0, 0, -1), (1, 2, 1, -1), (0, 2, 0, 0), (1, 2, 1, 1), (0, 3, 1, 3),
             (3, 0, 1, -1), (3, 0, 1, 2),
         ),
         (
-            (2, 1, 0, 0), (0, 0, 1, 1), (3, 1, 1, -1), (3, 2, 0, -1), (3, 2, 0, 3), (3, 0, 0, -1),
-            (3, 0, 0, 2), (3, 3, 1, -1),
-        ),
-        (
-            (0, 0, 1, 0), (0, 2, 1, 1), (3, 3, 1, 3), (3, 2, 1, -1), (1, 2, 0, -1), (3, 3, 0, -1),
-        ),
-        (
-            (0, 3, 0, 0), (0, 3, 0, 1), (3, 2, 1, 3), (2, 0, 1, -1), (3, 1, 0, -1),
-        ),
-        (
-            (0, 3, 1, 0), (0, 3, 1, 1), (3, 3, 0, 3), (2, 2, 1, -1), (1, 0, 1, -1),
+            (3, 1, 1, -1), (3, 2, 0, -1), (2, 1, 0, 0), (0, 0, 1, 1), (3, 2, 0, 3), (3, 0, 0, -1),
+            (3, 0, 0, 2),
+        ),
+        (
+            (3, 3, 1, -1), (3, 2, 1, -1), (1, 2, 0, -1), (0, 0, 1, 0), (0, 2, 1, 1), (3, 3, 1, 3),
+        ),
+        (
+            (3, 3, 0, -1), (2, 0, 1, -1), (3, 1, 0, -1), (0, 3, 0, 0), (0, 3, 0, 1), (3, 2, 1, 3),
+        ),
+        (
+            (2, 2, 1, -1), (1, 0, 1, -1), (0, 3, 1, 0), (0, 3, 1, 1), (3, 3, 0, 3),
         ),
         (
             (2, 3, 0, -1), (1, 3, 0, -1),
@@ -96,12 +95,12 @@
         ((0, 0), (0, 1), (2, 0), (1, 0)),
         ((3, 0), (0, 2), (2, 1), (1, 1)),
         ((0, 3), (2, 2), (1, 2), (3, 1)),
-        ((3, 2), (2, 3), (1, 3), (3, 3)),
+        ((3, 2), (3, 3), (2, 3), (1, 3)),
     ),
     (
         ((0, 1), (0, 0), (0, 2), (2, 1)),
         ((1, 1), (0, 3), (3, 0), (1, 2)),
-        ((3, 2), (3, 3), (2, 0), (3, 1)),
+        ((3, 2), (2, 0), (3, 1), (3, 3)),
         ((2, 2), (1, 0), (2, 3), (1, 3)),
     ),
 )

time: 49.6 us -> 50.8 us (1.024)
  Pallas kernels: 48.2 us -> 49.3 us
    pallas_call x1, Pallas kernels: 48.2 us -> 49.3 us  [fused(): pl.pallas_call(functools.partial(kernel, orients, population), out_shape=...]
where the time goes in v4:
time: 50.8 us; the launch traced here: 50.6 us
  Pallas kernels  49.3 us (97%)
  local copies, waits for them, and re-layouts  1.26 us (2%)
    pallas_call x1, Pallas kernels, fused(): pl.pallas_call(functools.partial(kernel, orients, population), out_shape=...  49.3 us
    unnamed x1, local copies, waits for them, and re-layouts  1.26 us

profile of v4, /device:TPU:0, one launch (start us, length us, event | category | flops | bytes accessed | tf_op | source)
XLA Modules:
  0.0 50.6 jit_solution(60787886599469016)
XLA Ops:
  0.0 49.3 %shard_map.64 = f32[1,512]{1,0:T(1,128)} custom-call(bf16[1,32,4096]{2,1,0:T(8,128)(2,1)} %refs.1, bf16[512,4096]{1,0:T(8,128)(2,1)} %parts.1, s32[1,512]{1,0:T(1,128)} %bitcast.4, s32[1,512]{1,0:T(1,128)} %bitcast.5, s32[1,512]{1,0:T(1,128)} %bitcast.6, f32[1,512]{1,0:T(1,128)} %bitcast.7), custom_call_target="tpu_custom_call" | custom-call | flops 4294967296 | bytes 12582912 | tf_op jit(solution)/shard_map/pallas_call | solution.py:341
  49.3 1.3 %copy.8 = f32[1,512]{1,0:T(1,128)} copy(f32[1,512]{1,0:T(1,128)} %shard_map.64) | data formatting | bytes 4096

commit v5 on v2

--- a/solution.py
+++ b/solution.py
@@ -116,7 +116,7 @@
     rows, pv, cid, oid, off, wts, top_s, tot_s, cho_s, part, recv1, send2, recv2,
     local_sem, ici_sem, sib_sem, send_sem, r1_sem, r2_sem, s1_sem, s2_sem,
 ):
-    n_cls, n_ptl = part.shape[0], part.shape[1]
+    n_ptl, n_cls = part.shape[0], part.shape[1]
     voxels = refs.shape[2]
     half = pv.shape[1]
     cls, ptl = lax.axis_index("cls"), lax.axis_index("ptl")
@@ -254,8 +254,11 @@
     coef = jnp.where(which == code, gain, 0.0).astype(jnp.bfloat16)
     width = voxels // n_ptl
     lane = lax.broadcasted_iota(jnp.int32, (ROWS, 128), 1) % NX
-    for j in range(n_ptl):
-        pixels = pv[:, :, j * width : (j + 1) * width].reshape(2 * half, width)
+    copies = []
+    for o in range(1, n_ptl + 1):
+        owner = lax.rem(ptl + o, n_ptl)
+        columns = pl.ds(pl.multiple_of(owner * width, width), width)
+        pixels = pv[:, :, columns].reshape(2 * half, width)
         moved = jnp.dot(coef, pixels, preferred_element_type=jnp.float32)
         for v in range(width // 128):
             total = jnp.zeros((ROWS, 128), jnp.float32)
@@ -268,46 +271,44 @@
                 across = pltpu.roll(a, (step + NX) % 128, 1)
                 keep = lane >= step if step > 0 else lane < NX + step
                 total += jnp.where(keep, inside, across)
-            for c in range(n_cls):
-                part[c, j : j + 1, v * 128 : (v + 1) * 128] = total[c : c + 1]
-
-    copies = []
+            part[o - 1, :, v * 128 : (v + 1) * 128] = total[:n_cls]
+        if o < n_ptl:
+            copies.append(
+                pltpu.make_async_remote_copy(
+                    src_ref=part.at[o - 1],
+                    dst_ref=recv1.at[o - 1],
+                    send_sem=s1_sem.at[o - 1],
+                    recv_sem=r1_sem.at[o - 1],
+                    device_id=(cls, owner),
+                    device_id_type=MESH,
+                )
+            )
+            copies[-1].start()
+    mine = part[n_ptl - 1]
+    for o in range(1, n_ptl):
+        copies[o - 1].wait_recv()
+        mine += recv1[o - 1]
+    for c in range(n_cls):
+        send2[c] = mine[c : c + 1]
+    last = []
     for q in (1, 2, 3):
-        copies.append(
+        last.append(
             pltpu.make_async_remote_copy(
-                src_ref=part.at[column[q]],
-                dst_ref=recv1.at[q - 1],
-                send_sem=s1_sem.at[q - 1],
-                recv_sem=r1_sem.at[q - 1],
+                src_ref=send2.at[column[q]],
+                dst_ref=recv2.at[q - 1],
+                send_sem=s2_sem.at[q - 1],
+                recv_sem=r2_sem.at[q - 1],
                 device_id=(column[q], ptl),
                 device_id_type=MESH,
             )
         )
-        copies[-1].start()
-    for copy in copies:
-        copy.wait_recv()
-    mine = part[cls] + recv1[0] + recv1[1] + recv1[2]
-    for j in range(n_ptl):
-        send2[j] = mine[j : j + 1]
-    for o in range(1, n_ptl):
-        to = lax.rem(ptl + o, n_ptl)
-        copies.append(
-            pltpu.make_async_remote_copy(
-                src_ref=send2.at[to],
-                dst_ref=recv2.at[o - 1],
-                send_sem=s2_sem.at[o - 1],
-                recv_sem=r2_sem.at[o - 1],
-                device_id=(cls, to),
-                device_id_type=MESH,
-            )
-        )
-        copies[-1].start()
-    total = send2[ptl]
-    for o in range(1, n_ptl):
-        copies[2 + o].wait_recv()
-        total += recv2[o - 1]
+        last[-1].start()
+    total = send2[cls]
+    for q in (1, 2, 3):
+        last[q - 1].wait_recv()
+        total += recv2[q - 1]
     out[...] = total / jnp.sqrt(jnp.float32(population))
-    for copy in copies:
+    for copy in copies + last:
         copy.wait_send()
 
     def sent(count, idx):
@@ -351,18 +352,18 @@
             pltpu.VMEM((1, count), f32),
             pltpu.VMEM((1, count), f32),
             pltpu.VMEM((1, count), f32),
-            pltpu.VMEM((n_cls, n_ptl, voxels // n_ptl), f32),
-            pltpu.VMEM((n_cls - 1, n_ptl, voxels // n_ptl), f32),
-            pltpu.VMEM((n_ptl, 1, voxels // n_ptl), f32),
-            pltpu.VMEM((n_ptl - 1, 1, voxels // n_ptl), f32),
+            pltpu.VMEM((n_ptl, n_cls, voxels // n_ptl), f32),
+            pltpu.VMEM((n_ptl - 1, n_cls, voxels // n_ptl), f32),
+            pltpu.VMEM((n_cls, 1, voxels // n_ptl), f32),
+            pltpu.VMEM((n_cls - 1, 1, voxels // n_ptl), f32),
             pltpu.SemaphoreType.DMA((8,)),
             pltpu.SemaphoreType.DMA((n_cls * n_ptl // 2, 2)),
             pltpu.SemaphoreType.DMA((n_cls * n_ptl // 2, 2)),
             pltpu.SemaphoreType.DMA((5,)),
+            pltpu.SemaphoreType.DMA((n_ptl - 1,)),
             pltpu.SemaphoreType.DMA((n_cls - 1,)),
             pltpu.SemaphoreType.DMA((n_ptl - 1,)),
             pltpu.SemaphoreType.DMA((n_cls - 1,)),
-            pltpu.SemaphoreType.DMA((n_ptl - 1,)),
         ],
         compiler_params=pltpu.CompilerParams(
             collective_id=0, has_side_effects=True, vmem_limit_bytes=60 * 1024 * 1024

time: 49.6 us -> 50.1 us (1.010)
  no operation moved by 1% of the time
where the time goes in v5:
time: 50.1 us; the launch traced here: 49.9 us
  Pallas kernels  48.6 us (97%)
  local copies, waits for them, and re-layouts  1.26 us (3%)
    pallas_call x1, Pallas kernels, fused(): pl.pallas_call(functools.partial(kernel, orients, population), out_shape=...  48.6 us
    unnamed x1, local copies, waits for them, and re-layouts  1.26 us

profile of v5, /device:TPU:0, one launch (start us, length us, event | category | flops | bytes accessed | tf_op | source)
XLA Modules:
  0.0 49.9 jit_solution(14799076596490086131)
XLA Ops:
  0.0 48.6 %shard_map.64 = f32[1,512]{1,0:T(1,128)} custom-call(bf16[1,32,4096]{2,1,0:T(8,128)(2,1)} %refs.1, bf16[512,4096]{1,0:T(8,128)(2,1)} %parts.1, s32[1,512]{1,0:T(1,128)} %bitcast.4, s32[1,512]{1,0:T(1,128)} %bitcast.5, s32[1,512]{1,0:T(1,128)} %bitcast.6, f32[1,512]{1,0:T(1,128)} %bitcast.7), custom_call_target="tpu_custom_call" | custom-call | flops 4294967296 | bytes 12582912 | tf_op jit(solution)/shard_map/pallas_call | solution.py:343
  48.6 1.3 %copy.8 = f32[1,512]{1,0:T(1,128)} copy(f32[1,512]{1,0:T(1,128)} %shard_map.64) | data formatting | bytes 4096

commit v6 on v4

--- a/solution.py
+++ b/solution.py
@@ -15,97 +15,105 @@
 PLAN = (
     (
         (
-            (0, 0, 1, 0), (0, 0, 0, 1), (0, 0, 0, 2), (0, 0, 0, 0), (0, 0, 1, 1), (0, 0, 1, 2),
-        ),
-        (
-            (0, 1, 0, -1), (2, 0, 0, -1), (1, 0, 1, -1), (2, 0, 0, 0), (1, 0, 1, 1),
-        ),
-        (
-            (0, 1, 1, -1), (2, 0, 1, -1), (1, 0, 0, -1), (0, 1, 1, 0), (0, 1, 0, 1),
-        ),
-        (
-            (0, 2, 0, -1), (3, 0, 1, -1), (3, 0, 0, -1), (3, 0, 1, 2), (0, 1, 0, 0), (0, 1, 1, 1),
-        ),
-        (
-            (3, 0, 0, 2), (0, 2, 1, -1), (2, 1, 0, -1), (1, 1, 1, -1), (0, 2, 0, 0), (0, 2, 0, 1),
-        ),
-        (
-            (0, 3, 0, -1), (2, 1, 1, -1), (1, 1, 0, -1), (0, 2, 1, 0), (0, 2, 1, 1),
-        ),
-        (
-            (0, 3, 1, -1), (2, 2, 0, -1), (1, 2, 0, -1), (2, 1, 0, 0), (1, 1, 1, 1),
-        ),
-        (
-            (3, 2, 0, -1), (2, 2, 1, -1), (1, 2, 1, -1), (0, 3, 0, 0), (0, 3, 0, 1),
-        ),
-        (
-            (3, 3, 1, -1), (3, 1, 1, -1), (3, 1, 0, -1), (0, 3, 1, 0), (0, 3, 1, 1),
-        ),
-        (
-            (3, 2, 1, -1), (2, 3, 0, -1), (1, 3, 0, -1),
-        ),
-        (
-            (3, 3, 0, -1), (2, 3, 1, -1), (1, 3, 1, -1),
+            (0, 0, 2, 0), (0, 0, 0, 1), (0, 0, 0, 2),
+        ),
+        (
+            (0, 0, 3, 0), (0, 0, 1, 1), (0, 0, 1, 2), (0, 0, 0, 0), (0, 0, 2, 1), (0, 0, 2, 2),
+            (0, 1, 0, -1), (2, 0, 0, -1), (1, 0, 2, -1), (2, 0, 0, 0), (1, 0, 2, 1), (0, 0, 3, 2),
+            (0, 1, 1, -1), (2, 0, 1, -1), (1, 0, 3, -1), (2, 0, 1, 0), (1, 0, 3, 1), (0, 1, 2, -1),
+            (2, 0, 2, -1), (1, 0, 0, -1), (0, 1, 2, 0), (0, 1, 0, 1), (0, 1, 3, -1), (3, 0, 2, -1),
+            (3, 0, 0, -1), (3, 0, 2, 2), (0, 1, 3, 0), (0, 1, 1, 1), (3, 0, 0, 2), (0, 2, 0, -1),
+            (3, 0, 3, -1), (3, 0, 1, -1), (0, 0, 1, 0), (0, 0, 3, 1), (3, 0, 3, 2), (0, 2, 1, -1),
+            (2, 1, 0, -1), (1, 1, 2, -1), (0, 1, 0, 0), (0, 1, 2, 1), (3, 0, 1, 2), (0, 2, 2, -1),
+            (2, 1, 1, -1), (1, 1, 3, -1), (0, 1, 1, 0), (0, 1, 3, 1), (0, 2, 3, -1), (2, 0, 3, -1),
+            (1, 0, 1, -1),
+        ),
+        (
+            (0, 2, 0, 0), (0, 2, 0, 1), (0, 3, 0, -1), (2, 1, 2, -1), (1, 1, 0, -1), (0, 2, 1, 0),
+            (0, 2, 1, 1), (0, 3, 1, -1), (2, 1, 3, -1), (1, 1, 1, -1),
+        ),
+        (
+            (2, 1, 0, 0), (1, 1, 2, 1), (0, 3, 2, -1), (2, 2, 0, -1), (1, 2, 0, -1),
+        ),
+        (
+            (0, 2, 2, 0), (0, 2, 2, 1), (0, 3, 3, -1), (2, 2, 1, -1), (1, 2, 1, -1),
+        ),
+        (
+            (2, 1, 1, 0), (1, 1, 3, 1), (3, 2, 0, -1), (3, 1, 2, -1), (3, 1, 0, -1), (0, 2, 3, 0),
+            (0, 2, 3, 1), (3, 3, 2, -1), (2, 2, 2, -1), (1, 2, 2, -1), (0, 3, 0, 0), (0, 3, 0, 1),
+            (3, 2, 2, -1), (3, 1, 3, -1), (3, 1, 1, -1), (0, 3, 1, 0), (0, 3, 1, 1), (3, 2, 1, -1),
+            (2, 2, 3, -1), (1, 2, 3, -1),
+        ),
+        (
+            (0, 3, 2, 0), (0, 3, 2, 1), (3, 3, 0, -1), (2, 3, 0, -1), (1, 3, 0, -1), (0, 3, 3, 0),
+            (0, 3, 3, 1), (3, 2, 3, -1), (2, 3, 1, -1), (1, 3, 1, -1),
+        ),
+        (
+            (3, 3, 3, -1), (2, 3, 2, -1), (1, 3, 2, -1), (3, 3, 1, -1), (2, 3, 3, -1), (1, 3, 3, -1),
         ),
     ),
     (
         (
-            (0, 1, 1, 0), (0, 1, 0, 1), (0, 1, 0, 2), (0, 1, 0, 3), (0, 1, 0, 0), (0, 1, 1, 1),
-            (0, 1, 1, 2), (0, 1, 1, 3),
-        ),
-        (
-            (0, 0, 0, -1), (0, 2, 0, -1), (2, 1, 0, -1), (1, 1, 1, -1), (0, 0, 0, 0), (0, 2, 0, 1),
-            (0, 0, 0, 2), (0, 2, 0, 3),
-        ),
-        (
-            (0, 0, 1, -1), (0, 2, 1, -1), (2, 1, 1, -1), (1, 1, 0, -1), (0, 2, 1, 0), (0, 0, 0, 1),
-            (0, 0, 1, 2), (0, 2, 1, 3),
-        ),
-        (
-            (0, 3, 0, -1), (2, 2, 0, -1), (1, 0, 0, -1), (2, 2, 0, 0), (1, 1, 1, 1), (0, 3, 0, 3),
-        ),
-        (
-            (0, 3, 1, -1), (2, 0, 0, -1), (1, 2, 1, -1), (0, 2, 0, 0), (1, 2, 1, 1), (0, 3, 1, 3),
-            (3, 0, 1, -1), (3, 0, 1, 2),
-        ),
-        (
-            (3, 1, 1, -1), (3, 2, 0, -1), (2, 1, 0, 0), (0, 0, 1, 1), (3, 2, 0, 3), (3, 0, 0, -1),
-            (3, 0, 0, 2),
-        ),
-        (
-            (3, 3, 1, -1), (3, 2, 1, -1), (1, 2, 0, -1), (0, 0, 1, 0), (0, 2, 1, 1), (3, 3, 1, 3),
-        ),
-        (
-            (3, 3, 0, -1), (2, 0, 1, -1), (3, 1, 0, -1), (0, 3, 0, 0), (0, 3, 0, 1), (3, 2, 1, 3),
-        ),
-        (
-            (2, 2, 1, -1), (1, 0, 1, -1), (0, 3, 1, 0), (0, 3, 1, 1), (3, 3, 0, 3),
-        ),
-        (
-            (2, 3, 0, -1), (1, 3, 0, -1),
-        ),
-        (
-            (2, 3, 1, -1), (1, 3, 1, -1),
+            (0, 1, 2, 0), (0, 1, 0, 1), (0, 1, 0, 2), (0, 1, 0, 3),
+        ),
+        (
+            (0, 1, 3, 0), (0, 1, 1, 1), (0, 1, 1, 2), (0, 1, 1, 3), (0, 1, 0, 0), (0, 1, 2, 1),
+            (0, 1, 2, 2), (0, 1, 2, 3), (0, 0, 0, -1), (0, 2, 0, -1), (2, 1, 0, -1), (1, 1, 2, -1),
+            (0, 1, 1, 0), (0, 2, 0, 1), (0, 1, 3, 2), (0, 1, 3, 3), (0, 0, 1, -1), (0, 2, 1, -1),
+            (2, 1, 1, -1), (1, 1, 3, -1), (0, 0, 0, 0), (0, 2, 1, 1), (0, 0, 0, 2), (0, 2, 0, 3),
+            (0, 0, 2, -1), (0, 2, 2, -1), (2, 1, 2, -1), (1, 1, 0, -1), (0, 2, 2, 0), (0, 1, 3, 1),
+            (0, 0, 1, 2), (0, 2, 1, 3), (0, 0, 3, -1), (0, 2, 3, -1), (2, 2, 0, -1), (1, 1, 1, -1),
+            (0, 2, 3, 0), (0, 0, 0, 1), (0, 0, 2, 2), (0, 2, 2, 3), (0, 3, 0, -1), (2, 2, 1, -1),
+            (1, 0, 0, -1), (2, 2, 0, 0), (1, 1, 2, 1), (0, 0, 3, 2), (0, 2, 3, 3), (0, 3, 1, -1),
+            (2, 1, 3, -1), (1, 2, 2, -1), (3, 0, 2, -1), (2, 2, 1, 0), (1, 2, 2, 1), (3, 0, 2, 2),
+            (0, 3, 0, 3), (0, 3, 2, -1), (2, 0, 0, -1), (1, 2, 3, -1), (3, 0, 0, -1), (0, 2, 0, 0),
+            (1, 2, 3, 1), (3, 0, 0, 2), (0, 3, 1, 3), (0, 3, 3, -1), (3, 1, 2, -1), (3, 2, 0, -1),
+            (3, 0, 3, -1),
+        ),
+        (
+            (2, 1, 0, 0), (0, 0, 1, 1), (3, 0, 3, 2), (0, 3, 2, 3), (3, 3, 2, -1), (3, 2, 2, -1),
+            (3, 2, 1, -1), (3, 0, 1, -1), (0, 0, 1, 0), (1, 1, 3, 1), (3, 0, 1, 2), (0, 3, 3, 3),
+            (3, 3, 0, -1), (3, 2, 3, -1), (1, 2, 0, -1),
+        ),
+        (
+            (0, 2, 1, 0), (0, 0, 2, 1), (3, 2, 0, 3), (3, 3, 3, -1), (2, 0, 1, -1), (3, 1, 0, -1),
+        ),
+        (
+            (2, 1, 1, 0), (0, 2, 2, 1), (3, 3, 2, 3), (3, 3, 1, -1), (3, 1, 3, -1), (1, 0, 1, -1),
+        ),
+        (
+            (0, 0, 2, 0), (0, 0, 3, 1), (3, 2, 2, 3), (2, 0, 2, -1), (1, 2, 1, -1), (0, 0, 3, 0),
+            (0, 2, 3, 1), (3, 2, 1, 3), (2, 2, 2, -1), (3, 1, 1, -1), (0, 3, 0, 0), (0, 3, 0, 1),
+            (3, 3, 0, 3), (2, 0, 3, -1), (1, 0, 2, -1), (0, 3, 1, 0), (0, 3, 1, 1), (3, 2, 3, 3),
+            (2, 2, 3, -1), (1, 0, 3, -1),
+        ),
+        (
+            (0, 3, 2, 0), (0, 3, 2, 1), (3, 3, 3, 3), (2, 3, 0, -1), (1, 3, 0, -1), (0, 3, 3, 0),
+            (0, 3, 3, 1), (3, 3, 1, 3), (2, 3, 1, -1), (1, 3, 1, -1),
+        ),
+        (
+            (2, 3, 2, -1), (1, 3, 2, -1), (2, 3, 3, -1), (1, 3, 3, -1),
         ),
     ),
 )
 
 GROUPS = (
     (
-        ((0, 0), (0, 1), (2, 0), (1, 0)),
-        ((3, 0), (0, 2), (2, 1), (1, 1)),
-        ((0, 3), (2, 2), (1, 2), (3, 1)),
+        ((0, 0), (0, 1), (3, 0), (2, 0)),
+        ((1, 0), (0, 2), (2, 1), (1, 1)),
+        ((0, 3), (3, 1), (2, 2), (1, 2)),
         ((3, 2), (3, 3), (2, 3), (1, 3)),
     ),
     (
-        ((0, 1), (0, 0), (0, 2), (2, 1)),
-        ((1, 1), (0, 3), (3, 0), (1, 2)),
-        ((3, 2), (2, 0), (3, 1), (3, 3)),
+        ((0, 1), (0, 0), (0, 2), (1, 1)),
+        ((2, 1), (0, 3), (3, 0), (3, 2)),
+        ((3, 3), (1, 2), (3, 1), (2, 0)),
         ((2, 2), (1, 0), (2, 3), (1, 3)),
     ),
 )
-UNITS = ((), (), ((0, 0),), ((0, 1),), (), (), ((1, 0),), ((1, 1),), ((2, 0),), ((2, 1),), ((3, 0), (3, 1)))
+UNITS = ((), ((0, 0),), ((0, 1),), ((1, 0),), ((1, 1),), ((2, 0),), ((2, 1),), ((3, 0), (3, 1)))
 DEPTH = 1024
+PARTS = 4
 ROWS = 8
 
 
@@ -161,13 +169,19 @@
         load.start()
     pl.semaphore_wait(barrier, 3 + n_ptl - 1)
 
+    def chunk(p, c, h):
+        return rows.at[p, c, h // 2, :, pl.ds(h % 2 * (voxels // 2), voxels // 2)]
+
+    def own_chunk(h):
+        return refs.at[0, pl.ds(16 * (h // 2), 16), pl.ds(h % 2 * (voxels // 2), voxels // 2)]
+
     def send(src, p, h, way):
         target, recv, idx = (
             (sibling, sib_sem, 4) if way == 4 else (ways[way], ici_sem, way)
         )
         pltpu.make_async_remote_copy(
             src_ref=src,
-            dst_ref=rows.at[p, core, h],
+            dst_ref=chunk(p, core, h),
             send_sem=send_sem.at[idx],
             recv_sem=recv.at[p, h],
             device_id=target,
@@ -177,12 +191,12 @@
     def run(section, zc):
         for q, zz, h, way in section:
             p = pair(q, zz)
-            block = rows.at[p, core, h]
+            block = chunk(p, core, h)
             if way < 0:
                 pltpu.make_async_copy(block, block, ici_sem.at[p, h]).wait()
                 send(block, p, h, 4)
             elif q == 0 and zz == zc:
-                send(refs.at[0, pl.ds(16 * h, 16)], p, h, way)
+                send(own_chunk(h), p, h, way)
             else:
                 send(block, p, h, way)
 
@@ -230,8 +244,8 @@
             def branch(s=s, zc=zc):
                 run(PLAN[zc][s], zc)
                 if s == 0:
-                    for h in range(2):
-                        send(refs.at[0, pl.ds(16 * h, 16)], own, h, 4)
+                    for h in range(PARTS):
+                        send(own_chunk(h), own, h, 4)
 
             pl.when(place == zc)(branch)
         if s == 0:
@@ -240,8 +254,8 @@
         for g, n in units:
             if n == 0:
                 for p in groups[g]:
-                    for h in range(2):
-                        block = rows.at[p, 1 - core, h]
+                    for h in range(PARTS):
+                        block = chunk(p, 1 - core, h)
                         pltpu.make_async_copy(block, block, sib_sem.at[p, h]).wait()
             scores(n, groups[g])
 
@@ -355,8 +369,8 @@
             pltpu.VMEM((n_ptl, 1, voxels // n_ptl), f32),
             pltpu.VMEM((n_ptl - 1, 1, voxels // n_ptl), f32),
             pltpu.SemaphoreType.DMA((8,)),
-            pltpu.SemaphoreType.DMA((n_cls * n_ptl // 2, 2)),
-            pltpu.SemaphoreType.DMA((n_cls * n_ptl // 2, 2)),
+            pltpu.SemaphoreType.DMA((n_cls * n_ptl // 2, PARTS)),
+            pltpu.SemaphoreType.DMA((n_cls * n_ptl // 2, PARTS)),
             pltpu.SemaphoreType.DMA((5,)),
             pltpu.SemaphoreType.DMA((n_cls - 1,)),
             pltpu.SemaphoreType.DMA((n_ptl - 1,)),

time: 50.8 us -> 53.8 us (1.059)
  Pallas kernels: 49.3 us -> 52.4 us
    pallas_call x1, Pallas kernels: 49.3 us -> 52.4 us  [fused(): pl.pallas_call(functools.partial(kernel, orients, population), out_shape=...]
where the time goes in v6:
time: 53.8 us; the launch traced here: 53.7 us
  Pallas kernels  52.4 us (97%)
  local copies, waits for them, and re-layouts  1.26 us (2%)
    pallas_call x1, Pallas kernels, fused(): pl.pallas_call(functools.partial(kernel, orients, population), out_shape=...  52.4 us
    unnamed x1, local copies, waits for them, and re-layouts  1.26 us

profile of v6, /device:TPU:0, one launch (start us, length us, event | category | flops | bytes accessed | tf_op | source)
XLA Modules:
  0.0 53.7 jit_solution(15508247029401858966)
XLA Ops:
  0.0 52.4 %shard_map.64 = f32[1,512]{1,0:T(1,128)} custom-call(bf16[1,32,4096]{2,1,0:T(8,128)(2,1)} %refs.1, bf16[512,4096]{1,0:T(8,128)(2,1)} %parts.1, s32[1,512]{1,0:T(1,128)} %bitcast.4, s32[1,512]{1,0:T(1,128)} %bitcast.5, s32[1,512]{1,0:T(1,128)} %bitcast.6, f32[1,512]{1,0:T(1,128)} %bitcast.7), custom_call_target="tpu_custom_call" | custom-call | flops 4294967296 | bytes 12582912 | tf_op jit(solution)/shard_map/pallas_call | solution.py:355
  52.4 1.3 %copy.8 = f32[1,512]{1,0:T(1,128)} copy(f32[1,512]{1,0:T(1,128)} %shard_map.64) | data formatting | bytes 4096

commit v7 on v4

--- a/solution.py
+++ b/solution.py
@@ -18,34 +18,32 @@
             (0, 0, 1, 0), (0, 0, 0, 1), (0, 0, 0, 2), (0, 0, 0, 0), (0, 0, 1, 1), (0, 0, 1, 2),
         ),
         (
-            (0, 1, 0, -1), (2, 0, 0, -1), (1, 0, 1, -1), (2, 0, 0, 0), (1, 0, 1, 1),
-        ),
-        (
-            (0, 1, 1, -1), (2, 0, 1, -1), (1, 0, 0, -1), (0, 1, 1, 0), (0, 1, 0, 1),
-        ),
-        (
-            (0, 2, 0, -1), (3, 0, 1, -1), (3, 0, 0, -1), (3, 0, 1, 2), (0, 1, 0, 0), (0, 1, 1, 1),
-        ),
-        (
-            (3, 0, 0, 2), (0, 2, 1, -1), (2, 1, 0, -1), (1, 1, 1, -1), (0, 2, 0, 0), (0, 2, 0, 1),
-        ),
-        (
-            (0, 3, 0, -1), (2, 1, 1, -1), (1, 1, 0, -1), (0, 2, 1, 0), (0, 2, 1, 1),
-        ),
-        (
-            (0, 3, 1, -1), (2, 2, 0, -1), (1, 2, 0, -1), (2, 1, 0, 0), (1, 1, 1, 1),
-        ),
-        (
-            (3, 2, 0, -1), (2, 2, 1, -1), (1, 2, 1, -1), (0, 3, 0, 0), (0, 3, 0, 1),
-        ),
-        (
-            (3, 3, 1, -1), (3, 1, 1, -1), (3, 1, 0, -1), (0, 3, 1, 0), (0, 3, 1, 1),
-        ),
-        (
-            (3, 2, 1, -1), (2, 3, 0, -1), (1, 3, 0, -1),
-        ),
-        (
-            (3, 3, 0, -1), (2, 3, 1, -1), (1, 3, 1, -1),
+            (0, 1, 0, -1), (2, 0, 0, -1), (1, 0, 1, -1), (2, 0, 0, 0), (1, 0, 1, 1), (0, 1, 0, 1),
+            (0, 1, 1, -1), (2, 0, 1, -1), (1, 0, 0, -1), (0, 1, 1, 0), (0, 1, 0, 4), (2, 0, 0, 4),
+            (1, 0, 0, 4),
+        ),
+        (
+            (0, 1, 0, 0), (0, 1, 1, 1),
+        ),
+        (
+            (0, 2, 0, -1), (3, 0, 1, -1), (3, 0, 0, -1), (3, 0, 1, 2), (3, 0, 0, 2), (3, 0, 0, 4),
+            (0, 2, 0, 0), (0, 2, 0, 1), (0, 2, 1, -1), (2, 1, 0, -1), (1, 1, 1, -1), (0, 2, 0, 4),
+            (0, 2, 1, 0), (0, 2, 1, 1), (0, 3, 0, -1), (2, 1, 1, -1), (1, 1, 0, -1), (2, 1, 0, 4),
+            (1, 1, 0, 4), (2, 1, 0, 0), (1, 1, 1, 1), (0, 3, 1, -1), (2, 2, 0, -1), (1, 2, 0, -1),
+            (0, 3, 0, 4),
+        ),
+        (
+            (0, 3, 0, 0), (0, 3, 0, 1),
+        ),
+        (
+            (3, 2, 0, -1), (2, 2, 1, -1), (1, 2, 1, -1), (2, 2, 0, 4), (1, 2, 0, 4), (0, 3, 1, 0),
+            (0, 3, 1, 1), (3, 2, 1, -1), (3, 1, 1, -1), (3, 1, 0, -1), (3, 2, 0, 4), (3, 1, 0, 4),
+        ),
+        (
+        ),
+        (
+            (3, 3, 1, -1), (2, 3, 0, -1), (1, 3, 0, -1), (3, 3, 0, -1), (2, 3, 1, -1), (1, 3, 1, -1),
+            (3, 3, 0, 4), (2, 3, 0, 4), (1, 3, 0, 4),
         ),
     ),
     (
@@ -55,37 +53,32 @@
         ),
         (
             (0, 0, 0, -1), (0, 2, 0, -1), (2, 1, 0, -1), (1, 1, 1, -1), (0, 0, 0, 0), (0, 2, 0, 1),
-            (0, 0, 0, 2), (0, 2, 0, 3),
-        ),
-        (
-            (0, 0, 1, -1), (0, 2, 1, -1), (2, 1, 1, -1), (1, 1, 0, -1), (0, 2, 1, 0), (0, 0, 0, 1),
-            (0, 0, 1, 2), (0, 2, 1, 3),
-        ),
-        (
-            (0, 3, 0, -1), (2, 2, 0, -1), (1, 0, 0, -1), (2, 2, 0, 0), (1, 1, 1, 1), (0, 3, 0, 3),
-        ),
-        (
-            (0, 3, 1, -1), (2, 0, 0, -1), (1, 2, 1, -1), (0, 2, 0, 0), (1, 2, 1, 1), (0, 3, 1, 3),
-            (3, 0, 1, -1), (3, 0, 1, 2),
-        ),
-        (
-            (3, 1, 1, -1), (3, 2, 0, -1), (2, 1, 0, 0), (0, 0, 1, 1), (3, 2, 0, 3), (3, 0, 0, -1),
-            (3, 0, 0, 2),
-        ),
-        (
-            (3, 3, 1, -1), (3, 2, 1, -1), (1, 2, 0, -1), (0, 0, 1, 0), (0, 2, 1, 1), (3, 3, 1, 3),
-        ),
-        (
-            (3, 3, 0, -1), (2, 0, 1, -1), (3, 1, 0, -1), (0, 3, 0, 0), (0, 3, 0, 1), (3, 2, 1, 3),
-        ),
-        (
-            (2, 2, 1, -1), (1, 0, 1, -1), (0, 3, 1, 0), (0, 3, 1, 1), (3, 3, 0, 3),
-        ),
-        (
-            (2, 3, 0, -1), (1, 3, 0, -1),
-        ),
-        (
-            (2, 3, 1, -1), (1, 3, 1, -1),
+            (0, 0, 0, 2), (0, 2, 0, 3), (0, 0, 0, 1), (0, 0, 1, -1), (0, 2, 1, -1), (2, 1, 1, -1),
+            (1, 1, 0, -1), (0, 2, 1, 0), (0, 0, 1, 2), (0, 2, 1, 3), (0, 0, 0, 4), (0, 2, 0, 4),
+            (2, 1, 0, 4), (1, 1, 0, 4),
+        ),
+        (
+            (1, 1, 1, 1),
+        ),
+        (
+            (0, 3, 0, -1), (2, 2, 0, -1), (1, 0, 0, -1), (2, 2, 0, 0), (0, 3, 0, 3), (0, 2, 0, 0),
+            (0, 3, 1, -1), (2, 0, 0, -1), (1, 2, 1, -1), (1, 2, 1, 1), (0, 3, 1, 3), (0, 3, 0, 4),
+            (2, 1, 0, 0), (0, 0, 1, 1), (3, 0, 1, -1), (3, 0, 1, 2), (3, 1, 1, -1), (3, 2, 0, -1),
+            (3, 2, 0, 3), (0, 0, 1, 0), (0, 2, 1, 1), (3, 0, 0, -1), (3, 0, 0, 2), (3, 0, 0, 4),
+            (3, 2, 1, -1), (1, 2, 0, -1), (3, 2, 1, 3), (1, 2, 0, 4), (3, 2, 0, 4),
+        ),
+        (
+            (0, 3, 0, 0), (0, 3, 0, 1), (3, 3, 1, -1), (3, 3, 1, 3),
+        ),
+        (
+            (2, 0, 1, -1), (3, 1, 0, -1), (2, 0, 0, 4), (3, 1, 0, 4), (0, 3, 1, 0), (0, 3, 1, 1),
+            (3, 3, 0, -1), (3, 3, 0, 3), (3, 3, 0, 4), (2, 2, 1, -1), (1, 0, 1, -1), (2, 2, 0, 4),
+            (1, 0, 0, 4),
+        ),
+        (
+        ),
+        (
+            (2, 3, 0, -1), (1, 3, 0, -1), (2, 3, 1, -1), (1, 3, 1, -1), (2, 3, 0, 4), (1, 3, 0, 4),
         ),
     ),
 )
@@ -94,8 +87,8 @@
     (
         ((0, 0), (0, 1), (2, 0), (1, 0)),
         ((3, 0), (0, 2), (2, 1), (1, 1)),
-        ((0, 3), (2, 2), (1, 2), (3, 1)),
-        ((3, 2), (3, 3), (2, 3), (1, 3)),
+        ((0, 3), (2, 2), (1, 2), (3, 2)),
+        ((3, 1), (3, 3), (2, 3), (1, 3)),
     ),
     (
         ((0, 1), (0, 0), (0, 2), (2, 1)),
@@ -104,7 +97,7 @@
         ((2, 2), (1, 0), (2, 3), (1, 3)),
     ),
 )
-UNITS = ((), (), ((0, 0),), ((0, 1),), (), (), ((1, 0),), ((1, 1),), ((2, 0),), ((2, 1),), ((3, 0), (3, 1)))
+UNITS = ((), ((0, 0),), ((0, 1),), ((1, 0),), ((1, 1),), ((2, 0),), ((2, 1),), ((3, 0), (3, 1)))
 DEPTH = 1024
 ROWS = 8
 
@@ -126,12 +119,12 @@
     along_x = cls + 1 - 2 * (cls % 2)
     along_y = cls + 2 - 4 * (cls // 2)
     column = (cls, along_x, along_y, 3 - cls)
-    sibling = (cls, ptl + 1 - 2 * core)
     ways = (
         (along_x, ptl),
         (along_y, ptl),
         (cls, ptl + 2 * sign),
         (cls, ptl - 2 * sign),
+        (cls, ptl + 1 - 2 * core),
     )
 
     def pair(q, zz):
@@ -149,38 +142,34 @@
         for i in range(2)
     ]
     own = cls * 4 + z
-    for h in range(2):
-        loads.append(
-            pltpu.make_async_copy(
-                refs.at[0, pl.ds(16 * h, 16)], rows.at[own, core, h], local_sem.at[2 + h]
-            )
-        )
+    loads.append(pltpu.make_async_copy(refs.at[0], rows.at[own, core], local_sem.at[2]))
     for i, (a, b) in enumerate(((cid_in, cid), (oid_in, oid), (off_in, off), (wts_in, wts))):
-        loads.append(pltpu.make_async_copy(a, b, local_sem.at[4 + i]))
+        loads.append(pltpu.make_async_copy(a, b, local_sem.at[3 + i]))
     for load in loads:
         load.start()
     pl.semaphore_wait(barrier, 3 + n_ptl - 1)
 
+    def chunk(p, h):
+        return rows.at[p, core, pl.ds(16 * h, 16)]
+
     def send(src, p, h, way):
-        target, recv, idx = (
-            (sibling, sib_sem, 4) if way == 4 else (ways[way], ici_sem, way)
-        )
         pltpu.make_async_remote_copy(
             src_ref=src,
-            dst_ref=rows.at[p, core, h],
-            send_sem=send_sem.at[idx],
-            recv_sem=recv.at[p, h],
-            device_id=target,
+            dst_ref=chunk(p, h) if way < 4 else rows.at[p, core],
+            send_sem=send_sem.at[way],
+            recv_sem=ici_sem.at[p, h] if way < 4 else sib_sem.at[p],
+            device_id=ways[way],
             device_id_type=MESH,
         ).start()
 
     def run(section, zc):
         for q, zz, h, way in section:
             p = pair(q, zz)
-            block = rows.at[p, core, h]
+            block = chunk(p, h)
             if way < 0:
                 pltpu.make_async_copy(block, block, ici_sem.at[p, h]).wait()
-                send(block, p, h, 4)
+            elif way == 4:
+                send(rows.at[p, core], p, h, way)
             elif q == 0 and zz == zc:
                 send(refs.at[0, pl.ds(16 * h, 16)], p, h, way)
             else:
@@ -194,7 +183,7 @@
         acc = jnp.zeros((len(group) * 64, half), jnp.float32)
         for k in range(0, voxels, DEPTH):
             lhs = jnp.concatenate(
-                [rows[p, :, :, :, k : k + DEPTH].reshape(64, DEPTH) for p in group], axis=0
+                [rows[p, :, :, k : k + DEPTH].reshape(64, DEPTH) for p in group], axis=0
             )
             acc += lax.dot_general(
                 lhs,
@@ -230,8 +219,7 @@
             def branch(s=s, zc=zc):
                 run(PLAN[zc][s], zc)
                 if s == 0:
-                    for h in range(2):
-                        send(refs.at[0, pl.ds(16 * h, 16)], own, h, 4)
+                    send(refs.at[0], own, 0, 4)
 
             pl.when(place == zc)(branch)
         if s == 0:
@@ -240,9 +228,8 @@
         for g, n in units:
             if n == 0:
                 for p in groups[g]:
-                    for h in range(2):
-                        block = rows.at[p, 1 - core, h]
-                        pltpu.make_async_copy(block, block, sib_sem.at[p, h]).wait()
+                    block = rows.at[p, 1 - core]
+                    pltpu.make_async_copy(block, block, sib_sem.at[p]).wait()
             scores(n, groups[g])
 
     gain = wts[...] * (n_cls * orients) * jnp.exp(cho_s[...] - top_s[...]) / tot_s[...]
@@ -344,7 +331,7 @@
         in_specs=[hbm] * 6,
         out_specs=vmem,
         scratch_shapes=[
-            pltpu.VMEM((n_cls * n_ptl // 2, 2, 2, local_ori // 2, voxels), references.dtype),
+            pltpu.VMEM((n_cls * n_ptl // 2, 2, local_ori, voxels), references.dtype),
             pltpu.VMEM((2, count // 2, voxels), particles.dtype),
             *[pltpu.VMEM((1, count), x.dtype) for x in line],
             pltpu.VMEM((1, count), f32),
@@ -354,9 +341,9 @@
             pltpu.VMEM((n_cls - 1, n_ptl, voxels // n_ptl), f32),
             pltpu.VMEM((n_ptl, 1, voxels // n_ptl), f32),
             pltpu.VMEM((n_ptl - 1, 1, voxels // n_ptl), f32),
-            pltpu.SemaphoreType.DMA((8,)),
+            pltpu.SemaphoreType.DMA((7,)),
             pltpu.SemaphoreType.DMA((n_cls * n_ptl // 2, 2)),
-            pltpu.SemaphoreType.DMA((n_cls * n_ptl // 2, 2)),
+            pltpu.SemaphoreType.DMA((n_cls * n_ptl // 2,)),
             pltpu.SemaphoreType.DMA((5,)),
             pltpu.SemaphoreType.DMA((n_cls - 1,)),
             pltpu.SemaphoreType.DMA((n_ptl - 1,)),

time: 50.8 us -> 50.6 us (level)
  no operation moved by 1% of the time
where the time goes in v7:
time: 50.6 us; the launch traced here: 50.4 us
  Pallas kernels  49.2 us (97%)
  local copies, waits for them, and re-layouts  1.26 us (2%)
    pallas_call x1, Pallas kernels, fused(): pl.pallas_call(functools.partial(kernel, orients, population), out_shape=...  49.2 us
    unnamed x1, local copies, waits for them, and re-layouts  1.26 us

profile of v7, /device:TPU:0, one launch (start us, length us, event | category | flops | bytes accessed | tf_op | source)
XLA Modules:
  0.0 50.4 jit_solution(8814760587905195488)
XLA Ops:
  0.0 49.2 %shard_map.64 = f32[1,512]{1,0:T(1,128)} custom-call(bf16[1,32,4096]{2,1,0:T(8,128)(2,1)} %refs.1, bf16[512,4096]{1,0:T(8,128)(2,1)} %parts.1, s32[1,512]{1,0:T(1,128)} %bitcast.4, s32[1,512]{1,0:T(1,128)} %bitcast.5, s32[1,512]{1,0:T(1,128)} %bitcast.6, f32[1,512]{1,0:T(1,128)} %bitcast.7), custom_call_target="tpu_custom_call" | custom-call | flops 4294967296 | bytes 12582912 | tf_op jit(solution)/shard_map/pallas_call | solution.py:328
  49.2 1.3 %copy.8 = f32[1,512]{1,0:T(1,128)} copy(f32[1,512]{1,0:T(1,128)} %shard_map.64) | data formatting | bytes 4096

commit v8 on v4

--- a/solution.py
+++ b/solution.py
@@ -18,28 +18,29 @@
             (0, 0, 1, 0), (0, 0, 0, 1), (0, 0, 0, 2), (0, 0, 0, 0), (0, 0, 1, 1), (0, 0, 1, 2),
         ),
         (
-            (0, 1, 0, -1), (2, 0, 0, -1), (1, 0, 1, -1), (2, 0, 0, 0), (1, 0, 1, 1),
-        ),
-        (
-            (0, 1, 1, -1), (2, 0, 1, -1), (1, 0, 0, -1), (0, 1, 1, 0), (0, 1, 0, 1),
-        ),
-        (
-            (0, 2, 0, -1), (3, 0, 1, -1), (3, 0, 0, -1), (3, 0, 1, 2), (0, 1, 0, 0), (0, 1, 1, 1),
-        ),
-        (
-            (3, 0, 0, 2), (0, 2, 1, -1), (2, 1, 0, -1), (1, 1, 1, -1), (0, 2, 0, 0), (0, 2, 0, 1),
-        ),
-        (
-            (0, 3, 0, -1), (2, 1, 1, -1), (1, 1, 0, -1), (0, 2, 1, 0), (0, 2, 1, 1),
-        ),
-        (
-            (0, 3, 1, -1), (2, 2, 0, -1), (1, 2, 0, -1), (2, 1, 0, 0), (1, 1, 1, 1),
-        ),
-        (
-            (3, 2, 0, -1), (2, 2, 1, -1), (1, 2, 1, -1), (0, 3, 0, 0), (0, 3, 0, 1),
-        ),
-        (
-            (3, 3, 1, -1), (3, 1, 1, -1), (3, 1, 0, -1), (0, 3, 1, 0), (0, 3, 1, 1),
+            (0, 1, 0, -1), (2, 0, 0, -1), (1, 0, 1, -1), (2, 0, 0, 0), (1, 0, 1, 1), (0, 1, 0, 1),
+        ),
+        (
+            (0, 1, 0, 0), (0, 1, 1, -1), (2, 0, 1, -1), (1, 0, 0, -1), (0, 1, 1, 0), (0, 1, 1, 1),
+        ),
+        (
+            (0, 2, 0, -1), (3, 0, 1, -1), (3, 0, 0, -1), (3, 0, 1, 2), (3, 0, 0, 2), (0, 2, 0, 0),
+            (0, 2, 0, 1),
+        ),
+        (
+            (0, 2, 1, -1), (2, 1, 0, -1), (1, 1, 1, -1), (0, 2, 1, 0), (0, 2, 1, 1),
+        ),
+        (
+            (2, 1, 0, 0), (1, 1, 1, 1), (0, 3, 0, -1), (2, 1, 1, -1), (1, 1, 0, -1),
+        ),
+        (
+            (0, 3, 0, 0), (0, 3, 0, 1), (0, 3, 1, -1), (2, 2, 0, -1), (1, 2, 0, -1),
+        ),
+        (
+            (0, 3, 1, 0), (0, 3, 1, 1), (3, 2, 0, -1), (2, 2, 1, -1), (1, 2, 1, -1),
+        ),
+        (
+            (3, 3, 1, -1), (3, 1, 1, -1), (3, 1, 0, -1),
         ),
         (
             (3, 2, 1, -1), (2, 3, 0, -1), (1, 3, 0, -1),
@@ -55,31 +56,31 @@
         ),
         (
             (0, 0, 0, -1), (0, 2, 0, -1), (2, 1, 0, -1), (1, 1, 1, -1), (0, 0, 0, 0), (0, 2, 0, 1),
-            (0, 0, 0, 2), (0, 2, 0, 3),
-        ),
-        (
-            (0, 0, 1, -1), (0, 2, 1, -1), (2, 1, 1, -1), (1, 1, 0, -1), (0, 2, 1, 0), (0, 0, 0, 1),
+            (0, 0, 0, 2), (0, 2, 0, 3), (0, 0, 0, 1),
+        ),
+        (
+            (1, 1, 1, 1), (0, 0, 1, -1), (0, 2, 1, -1), (2, 1, 1, -1), (1, 1, 0, -1), (0, 2, 1, 0),
             (0, 0, 1, 2), (0, 2, 1, 3),
         ),
         (
-            (0, 3, 0, -1), (2, 2, 0, -1), (1, 0, 0, -1), (2, 2, 0, 0), (1, 1, 1, 1), (0, 3, 0, 3),
-        ),
-        (
-            (0, 3, 1, -1), (2, 0, 0, -1), (1, 2, 1, -1), (0, 2, 0, 0), (1, 2, 1, 1), (0, 3, 1, 3),
-            (3, 0, 1, -1), (3, 0, 1, 2),
-        ),
-        (
-            (3, 1, 1, -1), (3, 2, 0, -1), (2, 1, 0, 0), (0, 0, 1, 1), (3, 2, 0, 3), (3, 0, 0, -1),
-            (3, 0, 0, 2),
-        ),
-        (
-            (3, 3, 1, -1), (3, 2, 1, -1), (1, 2, 0, -1), (0, 0, 1, 0), (0, 2, 1, 1), (3, 3, 1, 3),
-        ),
-        (
-            (3, 3, 0, -1), (2, 0, 1, -1), (3, 1, 0, -1), (0, 3, 0, 0), (0, 3, 0, 1), (3, 2, 1, 3),
-        ),
-        (
-            (2, 2, 1, -1), (1, 0, 1, -1), (0, 3, 1, 0), (0, 3, 1, 1), (3, 3, 0, 3),
+            (0, 2, 0, 0), (0, 3, 0, -1), (2, 2, 0, -1), (1, 0, 0, -1), (2, 2, 0, 0), (0, 3, 0, 3),
+        ),
+        (
+            (2, 1, 0, 0), (0, 0, 1, 1), (0, 3, 1, -1), (2, 0, 0, -1), (1, 2, 1, -1), (1, 2, 1, 1),
+            (0, 3, 1, 3), (3, 0, 1, -1), (3, 0, 1, 2),
+        ),
+        (
+            (0, 0, 1, 0), (0, 2, 1, 1), (3, 1, 1, -1), (3, 2, 0, -1), (3, 2, 0, 3), (3, 0, 0, -1),
+            (3, 0, 0, 2), (3, 3, 1, -1), (3, 3, 1, 3),
+        ),
+        (
+            (0, 3, 0, 0), (0, 3, 0, 1), (3, 2, 1, -1), (1, 2, 0, -1), (3, 2, 1, 3), (3, 3, 0, -1),
+        ),
+        (
+            (0, 3, 1, 0), (0, 3, 1, 1), (3, 3, 0, 3), (2, 0, 1, -1), (3, 1, 0, -1),
+        ),
+        (
+            (2, 2, 1, -1), (1, 0, 1, -1),
         ),
         (
             (2, 3, 0, -1), (1, 3, 0, -1),
@@ -100,7 +101,7 @@
     (
         ((0, 1), (0, 0), (0, 2), (2, 1)),
         ((1, 1), (0, 3), (3, 0), (1, 2)),
-        ((3, 2), (2, 0), (3, 1), (3, 3)),
+        ((3, 2), (3, 3), (2, 0), (3, 1)),
         ((2, 2), (1, 0), (2, 3), (1, 3)),
     ),
 )

time: 50.8 us -> 50.7 us (level)
  no operation moved by 1% of the time
where the time goes in v8:
time: 50.7 us; the launch traced here: 50.5 us
  Pallas kernels  49.2 us (97%)
  local copies, waits for them, and re-layouts  1.26 us (2%)
    pallas_call x1, Pallas kernels, fused(): pl.pallas_call(functools.partial(kernel, orients, population), out_shape=...  49.2 us
    unnamed x1, local copies, waits for them, and re-layouts  1.26 us

profile of v8, /device:TPU:0, one launch (start us, length us, event | category | flops | bytes accessed | tf_op | source)
XLA Modules:
  0.0 50.5 jit_solution(17858948351681179486)
XLA Ops:
  0.0 49.2 %shard_map.64 = f32[1,512]{1,0:T(1,128)} custom-call(bf16[1,32,4096]{2,1,0:T(8,128)(2,1)} %refs.1, bf16[512,4096]{1,0:T(8,128)(2,1)} %parts.1, s32[1,512]{1,0:T(1,128)} %bitcast.4, s32[1,512]{1,0:T(1,128)} %bitcast.5, s32[1,512]{1,0:T(1,128)} %bitcast.6, f32[1,512]{1,0:T(1,128)} %bitcast.7), custom_call_target="tpu_custom_call" | custom-call | flops 4294967296 | bytes 12582912 | tf_op jit(solution)/shard_map/pallas_call | solution.py:342
  49.2 1.3 %copy.8 = f32[1,512]{1,0:T(1,128)} copy(f32[1,512]{1,0:T(1,128)} %shard_map.64) | data formatting | bytes 4096

commit v9 on v2

--- a/solution.py
+++ b/solution.py
@@ -91,12 +91,12 @@
     ),
 )
 
-GROUPS = (
+BLOCKS = (
     (
         ((0, 0), (0, 1), (2, 0), (1, 0)),
         ((3, 0), (0, 2), (2, 1), (1, 1)),
         ((0, 3), (2, 2), (1, 2), (3, 1)),
-        ((3, 2), (2, 3), (1, 3), (3, 3)),
+        ((3, 2), (3, 3), (2, 3), (1, 3)),
     ),
     (
         ((0, 1), (0, 0), (0, 2), (2, 1)),
@@ -105,7 +105,24 @@
         ((2, 2), (1, 0), (2, 3), (1, 3)),
     ),
 )
-UNITS = ((), (), ((0, 0),), ((0, 1),), (), (), ((1, 0),), ((1, 1),), ((2, 0),), ((2, 1),), ((3, 0), (3, 1)))
+GROUPS = (
+    *(tuple((g, i, h) for i in range(4) for h in range(2)) for g in range(3)),
+    ((3, 0, 0), (3, 0, 1), (3, 1, 1), (3, 2, 0), (3, 3, 0)),
+    ((3, 1, 0), (3, 2, 1), (3, 3, 1)),
+)
+UNITS = (
+    (),
+    (),
+    ((0, 0),),
+    ((0, 1),),
+    (),
+    (),
+    ((1, 0),),
+    ((1, 1),),
+    ((2, 0), (2, 1)),
+    ((3, 0), (3, 1)),
+    ((4, 0), (4, 1)),
+)
 DEPTH = 1024
 ROWS = 8
 
@@ -192,10 +209,10 @@
     cho_s[...] = jnp.zeros(cho_s.shape, jnp.float32)
 
     def scores(n, group):
-        acc = jnp.zeros((len(group) * 64, half), jnp.float32)
+        acc = jnp.zeros((len(group) * 32, half), jnp.float32)
         for k in range(0, voxels, DEPTH):
             lhs = jnp.concatenate(
-                [rows[p, :, :, :, k : k + DEPTH].reshape(64, DEPTH) for p in group], axis=0
+                [rows[p, :, h, :, k : k + DEPTH].reshape(32, DEPTH) for p, h in group], axis=0
             )
             acc += lax.dot_general(
                 lhs,
@@ -212,19 +229,21 @@
             jnp.exp(sc - new), axis=0, keepdims=True
         )
         wanted = cid[:, cols] * orients + oid[:, cols]
-        inner = lax.broadcasted_iota(jnp.int32, (64, half), 0)
+        row = lax.broadcasted_iota(jnp.int32, (32, half), 0)
+        inner = row + row // 16 * 16
         picked = jnp.zeros((1, half), jnp.float32)
-        for i, p in enumerate(group):
-            mine = inner == wanted - p * 64
+        for i, (p, h) in enumerate(group):
+            mine = inner == wanted - (p * 64 + h * 16)
             picked += jnp.sum(
-                jnp.where(mine, sc[64 * i : 64 * i + 64], 0.0), axis=0, keepdims=True
+                jnp.where(mine, sc[32 * i : 32 * i + 32], 0.0), axis=0, keepdims=True
             )
         cho_s[:, cols] += picked
 
-    groups = [
+    places = [
         [jnp.where(place == 0, pair(*a), pair(*b)) for a, b in zip(first, second)]
-        for first, second in zip(*GROUPS)
+        for first, second in zip(*BLOCKS)
     ]
+    groups = [[(places[g][i], h) for g, i, h in group] for group in GROUPS]
     for s, units in enumerate(UNITS):
         for zc in range(2):
 
@@ -240,10 +259,9 @@
                 load.wait()
         for g, n in units:
             if n == 0:
-                for p in groups[g]:
-                    for h in range(2):
-                        block = rows.at[p, 1 - core, h]
-                        pltpu.make_async_copy(block, block, sib_sem.at[p, h]).wait()
+                for p, h in groups[g]:
+                    block = rows.at[p, 1 - core, h]
+                    pltpu.make_async_copy(block, block, sib_sem.at[p, h]).wait()
             scores(n, groups[g])
 
     gain = wts[...] * (n_cls * orients) * jnp.exp(cho_s[...] - top_s[...]) / tot_s[...]

time: 49.6 us -> 52.6 us (1.060)
  Pallas kernels: 48.2 us -> 51.1 us
    pallas_call x1, Pallas kernels: 48.2 us -> 51.1 us  [fused(): pl.pallas_call(functools.partial(kernel, orients, population), out_shape=...]
where the time goes in v9:
time: 52.6 us; the launch traced here: 52.4 us
  Pallas kernels  51.1 us (97%)
  local copies, waits for them, and re-layouts  1.26 us (2%)
    pallas_call x1, Pallas kernels, fused(): pl.pallas_call(functools.partial(kernel, orients, population), out_shape=...  51.1 us
    unnamed x1, local copies, waits for them, and re-layouts  1.26 us

profile of v9, /device:TPU:0, one launch (start us, length us, event | category | flops | bytes accessed | tf_op | source)
XLA Modules:
  0.0 52.4 jit_solution(3528611755119120563)
XLA Ops:
  0.0 51.1 %shard_map.64 = f32[1,512]{1,0:T(1,128)} custom-call(bf16[1,32,4096]{2,1,0:T(8,128)(2,1)} %refs.1, bf16[512,4096]{1,0:T(8,128)(2,1)} %parts.1, s32[1,512]{1,0:T(1,128)} %bitcast.4, s32[1,512]{1,0:T(1,128)} %bitcast.5, s32[1,512]{1,0:T(1,128)} %bitcast.6, f32[1,512]{1,0:T(1,128)} %bitcast.7), custom_call_target="tpu_custom_call" | custom-call | flops 4294967296 | bytes 12582912 | tf_op jit(solution)/shard_map/pallas_call | solution.py:360
  51.1 1.3 %copy.8 = f32[1,512]{1,0:T(1,128)} copy(f32[1,512]{1,0:T(1,128)} %shard_map.64) | data formatting | bytes 4096

commit v10 on v2

--- a/solution.py
+++ b/solution.py
@@ -105,7 +105,7 @@
         ((2, 2), (1, 0), (2, 3), (1, 3)),
     ),
 )
-UNITS = ((), (), ((0, 0),), ((0, 1),), (), (), ((1, 0),), ((1, 1),), ((2, 0),), ((2, 1),), ((3, 0), (3, 1)))
+UNITS = ((), (), (0,), (), (), (), (1,), (), (2,), (), (3,))
 DEPTH = 1024
 ROWS = 8
 
@@ -191,35 +191,34 @@
     tot_s[...] = jnp.zeros(tot_s.shape, jnp.float32)
     cho_s[...] = jnp.zeros(cho_s.shape, jnp.float32)
 
-    def scores(n, group):
-        acc = jnp.zeros((len(group) * 64, half), jnp.float32)
+    def scores(group):
+        acc = jnp.zeros((2 * half, len(group) * 64), jnp.float32)
         for k in range(0, voxels, DEPTH):
-            lhs = jnp.concatenate(
+            block = jnp.concatenate(
                 [rows[p, :, :, :, k : k + DEPTH].reshape(64, DEPTH) for p in group], axis=0
             )
             acc += lax.dot_general(
-                lhs,
-                pv[n, :, k : k + DEPTH],
+                pv[:, :, k : k + DEPTH].reshape(2 * half, DEPTH),
+                block,
                 (((1,), (1,)), ((), ())),
                 preferred_element_type=jnp.float32,
             )
-        sc = acc * (1.0 / math.sqrt(voxels))
-        cols = pl.ds(n * half, half)
-        old = top_s[:, cols]
+        sc = acc.T * (1.0 / math.sqrt(voxels))
+        old = top_s[...]
         new = jnp.maximum(old, jnp.max(sc, axis=0, keepdims=True))
-        top_s[:, cols] = new
-        tot_s[:, cols] = tot_s[:, cols] * jnp.exp(old - new) + jnp.sum(
+        top_s[...] = new
+        tot_s[...] = tot_s[...] * jnp.exp(old - new) + jnp.sum(
             jnp.exp(sc - new), axis=0, keepdims=True
         )
-        wanted = cid[:, cols] * orients + oid[:, cols]
-        inner = lax.broadcasted_iota(jnp.int32, (64, half), 0)
-        picked = jnp.zeros((1, half), jnp.float32)
+        wanted = cid[...] * orients + oid[...]
+        inner = lax.broadcasted_iota(jnp.int32, (64, 2 * half), 0)
+        picked = jnp.zeros((1, 2 * half), jnp.float32)
         for i, p in enumerate(group):
             mine = inner == wanted - p * 64
             picked += jnp.sum(
                 jnp.where(mine, sc[64 * i : 64 * i + 64], 0.0), axis=0, keepdims=True
             )
-        cho_s[:, cols] += picked
+        cho_s[...] += picked
 
     groups = [
         [jnp.where(place == 0, pair(*a), pair(*b)) for a, b in zip(first, second)]
@@ -238,13 +237,12 @@
         if s == 0:
             for load in loads:
                 load.wait()
-        for g, n in units:
-            if n == 0:
-                for p in groups[g]:
-                    for h in range(2):
-                        block = rows.at[p, 1 - core, h]
-                        pltpu.make_async_copy(block, block, sib_sem.at[p, h]).wait()
-            scores(n, groups[g])
+        for g in units:
+            for p in groups[g]:
+                for h in range(2):
+                    block = rows.at[p, 1 - core, h]
+                    pltpu.make_async_copy(block, block, sib_sem.at[p, h]).wait()
+            scores(groups[g])
 
     gain = wts[...] * (n_cls * orients) * jnp.exp(cho_s[...] - top_s[...]) / tot_s[...]
     gain = gain.astype(jnp.bfloat16).astype(jnp.float32)

time: 49.6 us -> 54.5 us (1.099)
  Pallas kernels: 48.2 us -> 53.1 us
    pallas_call x1, Pallas kernels: 48.2 us -> 53.1 us  [fused(): pl.pallas_call(functools.partial(kernel, orients, population), out_shape=...]
where the time goes in v10:
time: 54.5 us; the launch traced here: 54.4 us
  Pallas kernels  53.1 us (97%)
  local copies, waits for them, and re-layouts  1.26 us (2%)
    pallas_call x1, Pallas kernels, fused(): pl.pallas_call(functools.partial(kernel, orients, population), out_shape=...  53.1 us
    unnamed x1, local copies, waits for them, and re-layouts  1.26 us

profile of v10, /device:TPU:0, one launch (start us, length us, event | category | flops | bytes accessed | tf_op | source)
XLA Modules:
  0.0 54.4 jit_solution(516040506957481586)
XLA Ops:
  0.0 53.1 %shard_map.64 = f32[1,512]{1,0:T(1,128)} custom-call(bf16[1,32,4096]{2,1,0:T(8,128)(2,1)} %refs.1, bf16[512,4096]{1,0:T(8,128)(2,1)} %parts.1, s32[1,512]{1,0:T(1,128)} %bitcast.4, s32[1,512]{1,0:T(1,128)} %bitcast.5, s32[1,512]{1,0:T(1,128)} %bitcast.6, f32[1,512]{1,0:T(1,128)} %bitcast.7), custom_call_target="tpu_custom_call" | custom-call | flops 4294967296 | bytes 12582912 | tf_op jit(solution)/shard_map/pallas_call | solution.py:340
  53.1 1.3 %copy.8 = f32[1,512]{1,0:T(1,128)} copy(f32[1,512]{1,0:T(1,128)} %shard_map.64) | data formatting | bytes 4096
